TPU v7x, 256 devices: a whole 4x4x8 slice. The times are simulated.
256 devices in a mesh: patch: 64 (over x, z, y_hi), tensor: 4 (over y_lo, core).
Axes of the slice: x: 4, y: 4 (y_hi: 2, y_lo: 2; y = y_hi * 2 + y_lo), z: 8, core: 2. Of those that a mesh axis runs over, the one named last changes fastest.
Arguments:
- video: bfloat16 [17408, 3072], P('patch', 'tensor'), may hold values from -6 to 6
- positions: int32 [17408], P('patch'), may hold values from 0 to 17407, each once
- text_count: int32 [1], replicated, may hold values from 64 to 256
- mod_shift: float32 [3072], replicated, may hold values from -3 to 3
- mod_scale: float32 [3072], replicated, may hold values from -3 to 3
- gate: float32 [3072], P('tensor'), may hold values from 0.5 to 4
- w_query: bfloat16 [3072, 1536], P(None, 'tensor'), may hold values from -0.109375 to 0.109375
- w_key: bfloat16 [3072, 1536], P(None, 'tensor'), may hold values from -0.109375 to 0.109375
- w_value: bfloat16 [3072, 1536], P(None, 'tensor'), may hold values from -0.109375 to 0.109375
- w_out: bfloat16 [1536, 3072], P('tensor'), may hold values from -0.15625 to 0.15625
- q_gain: float32 [128], replicated, may hold values from 0.5 to 1.5
- k_gain: float32 [128], replicated, may hold values from 1.5 to 4
- stale_keys: bfloat16 [17408, 1536], P('patch', 'tensor'), as said below
- stale_values: bfloat16 [17408, 1536], P('patch', 'tensor'), may hold values from -6 to 6
- text_keys: bfloat16 [256, 1536], P(None, 'tensor'), may hold values from -16 to 16
- text_values: bfloat16 [256, 1536], P(None, 'tensor'), may hold values from -6 to 6
Outputs:
- mixed: float32 [17408, 3072], P('patch', 'tensor')
- fresh_keys: bfloat16 [17408, 1536], P('patch', 'tensor')
- fresh_values: bfloat16 [17408, 1536], P('patch', 'tensor')
Inputs may be any that keep to these rules, and one draw needn't show every extreme that they name: `positions`: each token's place in the clip, counted frame by frame, row by row; every place occurs once. Text slots from text_count on are padding. `stale_keys`: keys of the previous denoising step.
All inputs are finite; a program needn't handle non-finite values.
Results may differ from a plain program's by a relative error of at most 0.013.
The roundings to bfloat16 on the way count: a program that leaves them out, or rounds other values in their place, can miss the bound.
Values may be sent and summed in bfloat16 or wider, within the bound.
A program may use at most 128 MiB of HBM per device.

v0:
```python
import math

import jax
import jax.numpy as jnp
from jax import lax
from jax.sharding import PartitionSpec as P

HEAD_DIM = 128
TEXT = 256
GRID_H = 45
GRID_W = 80


EPSILON = 1e-06


def modulate(video, mod_shift, mod_scale):
    values = video.astype(jnp.float32)
    center = jnp.mean(values, axis=1, keepdims=True)
    spread = jnp.mean((values - center) ** 2, axis=1, keepdims=True)
    return ((values - center) * lax.rsqrt(spread + EPSILON) * (1.0 + mod_scale) + mod_shift).astype(
        jnp.bfloat16
    )


def head_norm(vectors, norm_gain):
    return (
        vectors
        * lax.rsqrt(jnp.mean(vectors * vectors, axis=-1, keepdims=True) + EPSILON)
        * norm_gain
    )


def rotate(vectors, positions):
    head_size = vectors.shape[-1]
    pair_count = head_size // 2
    time_pairs = head_size // 16
    height_pairs = (pair_count - time_pairs) // 2
    width_pairs = pair_count - time_pairs - height_pairs
    frame = (positions // (GRID_H * GRID_W)).astype(jnp.float32)
    height = (positions // GRID_W % GRID_H).astype(jnp.float32)
    across = (positions % GRID_W).astype(jnp.float32)

    def rates(number):
        return 256.0 ** (-jnp.arange(number, dtype=jnp.float32) / number)

    angles = jnp.concatenate(
        [
            frame[:, None] * rates(time_pairs)[None, :],
            height[:, None] * rates(height_pairs)[None, :],
            across[:, None] * rates(width_pairs)[None, :],
        ],
        axis=1,
    )
    cosine = jnp.cos(angles)[:, None, :]
    sine = jnp.sin(angles)[:, None, :]
    paired = vectors.reshape(vectors.shape[:-1] + (pair_count, 2))
    first_half = paired[..., 0]
    second_half = paired[..., 1]
    turned = jnp.stack(
        [first_half * cosine - second_half * sine, first_half * sine + second_half * cosine],
        axis=-1,
    )
    return turned.reshape(vectors.shape)


def project_heads(normed, weight, norm_gain, positions):
    heads = jnp.dot(normed, weight, preferred_element_type=jnp.float32)
    heads = heads.reshape(heads.shape[0], -1, HEAD_DIM)
    return rotate(head_norm(heads, norm_gain), positions).astype(jnp.bfloat16)


def absorb(state, queries, key_rows, value_rows, live):
    top_prev, totals, running = state
    count_keys = key_rows.shape[0]
    heads_here = queries.shape[1]
    factor = 1.0 / math.sqrt(HEAD_DIM)
    keys_split = key_rows.reshape(count_keys, heads_here, HEAD_DIM)
    values_split = value_rows.reshape(count_keys, heads_here, HEAD_DIM)
    scores = (
        jnp.einsum("qhd,khd->hqk", queries, keys_split, preferred_element_type=jnp.float32) * factor
    )
    scores = jnp.where(live[None, None, :], scores, -1e30)
    top_new = jnp.maximum(top_prev, jnp.max(scores, axis=-1))
    weights = jnp.where(live[None, None, :], jnp.exp(scores - top_new[:, :, None]), 0.0)
    rescale = jnp.exp(top_prev - top_new)
    totals = totals * rescale + jnp.sum(weights, axis=-1)
    added = jnp.einsum(
        "hqk,khd->qhd",
        weights.astype(jnp.bfloat16),
        values_split,
        preferred_element_type=jnp.float32,
    )
    running = running * jnp.transpose(rescale)[:, :, None] + added
    return (top_new, totals, running)


def absorb_blocks(state, queries, key_rows, value_rows, first_index, own_start):
    count_keys = key_rows.shape[0]
    block_rows = 1024
    block_count = count_keys // block_rows
    own_rows = queries.shape[0]
    key_blocks = key_rows.reshape(block_count, block_rows, key_rows.shape[1])
    value_blocks = value_rows.reshape(block_count, block_rows, value_rows.shape[1])
    offsets = jnp.arange(block_count, dtype=jnp.int32) * block_rows

    def advance(carry, items):
        key_part, value_part, offset = items
        index_rows = first_index + offset + jnp.arange(block_rows, dtype=jnp.int32)
        live = (index_rows < own_start) | (index_rows >= own_start + own_rows)
        return (absorb(carry, queries, key_part, value_part, live), None)

    state, unused = lax.scan(advance, state, (key_blocks, value_blocks, offsets))
    return state


def shards(
    video,
    positions,
    text_count,
    mod_shift,
    mod_scale,
    gate,
    w_query,
    w_key,
    w_value,
    w_out,
    q_gain,
    k_gain,
    stale_keys,
    stale_values,
    text_keys,
    text_values,
):
    row_count = video.shape[0]
    whole = lax.all_gather(video, "tensor", axis=1, tiled=True)
    normed = modulate(whole, mod_shift, mod_scale)
    queries = project_heads(normed, w_query, q_gain, positions)
    heads_here = queries.shape[1]
    fresh_keys = project_heads(normed, w_key, k_gain, positions).reshape(
        row_count, heads_here * HEAD_DIM
    )
    fresh_values = jnp.dot(normed, w_value, preferred_element_type=jnp.float32).astype(jnp.bfloat16)
    own_start = lax.axis_index("patch") * row_count
    start_state = (
        jnp.full((heads_here, row_count), -1e30, jnp.float32),
        jnp.zeros((heads_here, row_count), jnp.float32),
        jnp.zeros((row_count, heads_here, HEAD_DIM), jnp.float32),
    )
    first_keys = jnp.concatenate([fresh_keys, text_keys], axis=0)
    first_values = jnp.concatenate([fresh_values, text_values], axis=0)
    first_live = jnp.concatenate(
        [jnp.ones((row_count,), dtype=bool), jnp.arange(TEXT, dtype=jnp.int32) < text_count[0]]
    )
    state = absorb(start_state, queries, first_keys, first_values, first_live)
    every_keys, every_values = (
        lax.all_gather(stale_keys, "patch", axis=0, tiled=True),
        lax.all_gather(stale_values, "patch", axis=0, tiled=True),
    )
    state = absorb_blocks(state, queries, every_keys, every_values, 0, own_start)
    top_score, totals, running = state
    attended = (running / jnp.transpose(totals)[:, :, None]).astype(jnp.bfloat16)
    attended = attended.reshape(row_count, heads_here * HEAD_DIM)
    partial_terms = jnp.dot(attended, w_out, preferred_element_type=jnp.float32)
    branch = lax.psum_scatter(
        partial_terms.astype(jnp.bfloat16), "tensor", scatter_dimension=1, tiled=True
    ).astype(jnp.float32)
    mixed = video.astype(jnp.float32) + gate[None, :] * branch
    return (mixed, fresh_keys, fresh_values)


def solution(mesh):
    return jax.shard_map(
        shards,
        mesh=mesh,
        in_specs=(
            P("patch", "tensor"),
            P("patch"),
            P(),
            P(),
            P(),
            P("tensor"),
            P(None, "tensor"),
            P(None, "tensor"),
            P(None, "tensor"),
            P("tensor", None),
            P(),
            P(),
            P("patch", "tensor"),
            P("patch", "tensor"),
            P(None, "tensor"),
            P(None, "tensor"),
        ),
        out_specs=(P("patch", "tensor"), P("patch", "tensor"), P("patch", "tensor")),
        check_vma=False,
    )
```

profile of v0, /device:TPU:3, one launch (start us, length us, event | category | flops | bytes accessed | tf_op | source)
XLA Modules:
  0.0 623.6 jit_solution(15493479336565528361)
XLA Ops:
  18.7 22.7 %all-gather.4.cloned.1.call-done = bf16[272,3072]{1,0:T(8,128)(2,1)} async-done(((bf16[272,768]{1,0:T(8,128)(2,1)}), bf16[272,3072]{1,0:T(8,128)(2,1)}) %all-gather.4.cloned.1.call-update) | async-done | bytes 1671184 | tf_op jit(solution)/shard_map/all_gather | solution.py:136
  41.4 1.9 convert_reduce_fusion
  47.9 4.0 fusion.57
  52.5 4.0 fusion.56
  59.8 1.7 multiply_subtract_fusion
  63.3 2.1 copy.69
  69.1 1.7 fusion.27
  71.7 1.5 fusion.30
  73.2 149.4 %all-gather.6.cloned.1.call-done = bf16[17408,384]{1,0:T(8,128)(2,1)} async-done(((bf16[272,384]{1,0:T(8,128)(2,1)}), bf16[17408,384]{1,0:T(8,128)(2,1)}) %all-gather.6.cloned.1.call-update) | async-done | bytes 13369360 | tf_op jit(solution)/shard_map/all_gather | solution.py:157
  222.5 177.8 %all-gather.8.cloned.1.call-done = bf16[17408,384]{1,0:T(8,128)(2,1)} async-done(((bf16[272,384]{1,0:T(8,128)(2,1)}), bf16[17408,384]{1,0:T(8,128)(2,1)}) %all-gather.8.cloned.1.call-update) | async-done | bytes 13369360 | tf_op jit(solution)/shard_map/all_gather | solution.py:158
  400.3 186.4 %while.15 = (s32[]{:T(128)}, f32[3,272]{1,0:T(4,128)S(1)}, f32[3,272]{1,0:T(4,128)S(1)}, f32[272,3,128]{2,0,1:T(8,128)}, s32[17]{0:T(128)S(1)}, /*index=5*/s32[]...) while((s32[]{:T(128)}, f32[3,272]{1,0:T(4,128)S(1)}, ...), condition=%wide.region_9.10_spmd, body=%wide.region_6.9_spmd.sunk | while | flops 438897024 | bytes 25480420 | solution.py:113
  401.6 2.7 constant_dynamic-slice_fusion.3
  405.7 2.3 copy.98
  412.5 2.7 constant_dynamic-slice_fusion.3
  416.6 2.3 copy.98
  423.5 2.7 constant_dynamic-slice_fusion.3
  427.6 2.3 copy.98
  434.5 2.7 constant_dynamic-slice_fusion.3
  438.6 2.3 copy.98
  445.4 2.7 constant_dynamic-slice_fusion.3
  449.5 2.3 copy.98
  456.4 2.7 constant_dynamic-slice_fusion.3
  460.5 2.3 copy.98
  467.4 2.7 constant_dynamic-slice_fusion.3
  471.5 2.3 copy.98
  478.3 2.7 constant_dynamic-slice_fusion.3
  482.4 2.3 copy.98
  489.3 2.7 constant_dynamic-slice_fusion.3
  493.4 2.3 copy.98
  500.3 2.7 constant_dynamic-slice_fusion.3
  504.4 2.3 copy.98
  511.2 2.7 constant_dynamic-slice_fusion.3
  515.3 2.3 copy.98
  522.2 2.7 constant_dynamic-slice_fusion.3
  526.3 2.3 copy.98
  533.1 2.7 constant_dynamic-slice_fusion.3
  537.3 2.3 copy.98
  544.1 2.7 constant_dynamic-slice_fusion.3
  548.2 2.3 copy.98
  555.1 2.7 constant_dynamic-slice_fusion.3
  559.2 2.3 copy.98
  566.0 2.7 constant_dynamic-slice_fusion.3
  570.1 2.3 copy.98
  577.0 2.7 constant_dynamic-slice_fusion.3
  581.1 2.3 copy.98
  586.7 3.3 convolution_convert_fusion
  591.2 23.8 %reduce-scatter.2.cloned.1.call-done = bf16[272,768]{1,0:T(8,128)(2,1)} async-done(((bf16[272,3072]{1,0:T(8,128)(2,1)}), bf16[272,768]{1,0:T(8,128)(2,1)}) %reduce-scatter.2.cloned.1.call-update) | async-done | bytes 417808 | tf_op jit(solution)/shard_map/reduce_scatter | solution.py:165
  615.0 2.0 multiply_add_fusion.1
  (343 shorter events, 126.8 us)
Async XLA Ops:
  7.2 579.6 %copy-start = (bf16[384,3072]{1,0:T(8,128)(2,1)S(1)}, bf16[384,3072]{1,0:T(8,128)(2,1)}, u32[]{:S(2)}) copy-start(bf16[384,3072]{1,0:T(8,128)(2,1)} %param.27) | copy-start | bytes 7077892
  7.2 34.2 %all-gather.4.cloned.1.call-start = ((), (), s32[]{:S(2)}) async-start(), calls=%async_computation.1 | async-start | bytes 2088960 | tf_op jit(solution)/shard_map/all_gather | solution.py:136
  7.9 214.6 %all-gather.6.cloned.1.call-start = ((), (), s32[]{:S(2)}) async-start(), calls=%async_computation.2 | async-start | bytes 13578240 | tf_op jit(solution)/shard_map/all_gather | solution.py:157
  8.7 391.7 %all-gather.8.cloned.1.call-start = ((), (), s32[]{:S(2)}) async-start(), calls=%async_computation.3 | async-start | bytes 13578240 | tf_op jit(solution)/shard_map/all_gather | solution.py:158
  9.4 34.5 %copy-start.13 = (f32[3072]{0:T(1024)S(1)}, f32[3072]{0:T(1024)}, u32[]{:S(2)}) copy-start(f32[3072]{0:T(1024)} %param.21) | copy-start | bytes 36868
  9.4 605.6 %reduce-scatter.2.cloned.1.call-start = ((), (), s32[]{:S(2)}) async-start(), calls=%async_computation.4 | async-start | bytes 2088960 | tf_op jit(solution)/shard_map/reduce_scatter | solution.py:165
  41.4 1.9 copy-start.2
  43.3 1.7 copy-start.16
  45.0 1.2 copy-start.6
  45.0 1.9 copy-start.11
  61.5 5.3 copy-start.12
  62.2 5.7 copy-start.3
  62.2 4.9 copy-start.7
  62.2 4.9 copy-start.8
  66.8 2.3 copy-start.14
  69.1 2.6 copy-start.9
  71.7 328.7 %copy-start.19 = (s32[17]{0:T(128)S(1)}, s32[17]{0:T(128)}, u32[]{:S(2)}) copy-start(s32[17]{0:T(128)} %iota_multiply_fusion) | copy-start | bytes 208
  408.0 1.1 copy-start.1
  408.0 1.2 copy-start.17
  419.0 1.1 copy-start.1
  419.0 1.2 copy-start.17
  429.9 1.1 copy-start.1
  429.9 1.2 copy-start.17
  440.9 1.1 copy-start.1
  440.9 1.2 copy-start.17
  451.9 1.1 copy-start.1
  451.9 1.2 copy-start.17
  462.8 1.1 copy-start.1
  462.8 1.2 copy-start.17
  473.8 1.1 copy-start.1
  473.8 1.2 copy-start.17
  484.7 1.1 copy-start.1
  484.8 1.2 copy-start.17
  495.7 1.1 copy-start.1
  495.7 1.2 copy-start.17
  506.7 1.1 copy-start.1
  506.7 1.2 copy-start.17
  517.6 1.2 copy-start.17
  528.6 1.1 copy-start.1
  528.6 1.2 copy-start.17
  539.6 1.2 copy-start.17
  550.5 1.2 copy-start.17
  561.5 1.2 copy-start.17
  572.5 1.2 copy-start.17
  583.4 1.2 copy-start.17
  586.7 3.4 copy-start.4
  590.1 24.9 %copy-start.5 = (bf16[272,768]{1,0:T(8,128)(2,1)S(1)}, bf16[272,768]{1,0:T(8,128)(2,1)}, u32[]{:S(2)}) copy-start(bf16[272,768]{1,0:T(8,128)(2,1)} %param.18) | copy-start | bytes 1253380
  590.1 24.9 %copy-start.15 = (f32[768]{0:T(1024)S(1)}, f32[768]{0:T(1024)}, u32[]{:S(2)}) copy-start(f32[768]{0:T(1024)} %param.23) | copy-start | bytes 9220
  (24 other events, 25.1 us)
Sparse Core Ops, SparseCore 0:
  9.8 31.5 all-gather.3
  45.1 177.4 all-gather.5
  226.2 174.0 all-gather.7
  590.2 24.7 reduce-scatter.1
where the time goes:
time: 628 us; the launch traced here: 624 us
  waiting for transfers between devices  376 us (60%)
  local copies, waits for them, and re-layouts  143 us (23%)
  matrix products  45.3 us (7%)
  other arithmetic  43.9 us (7%)
  between operations  14.7 us (2%)
    all_gather x1, waiting for transfers between devices, shards(): lax.all_gather(stale_values, 'patch', axis=0, tiled=True)  178 us
    all_gather x1, waiting for transfers between devices, shards(): lax.all_gather(stale_keys, 'patch', axis=0, tiled=True)  149 us
    dynamic_slice x68, local copies, waits for them, and re-layouts, absorb_blocks(): lax.scan(advance, state, (key_blocks, value_blocks, offsets))  119 us
    reduce_scatter x1, waiting for transfers between devices, shards(): lax.psum_scatter(partial_terms.astype(jnp.bfloat16), 'tensor', scatter_di...  23.8 us
    all_gather x1, waiting for transfers between devices, shards(): whole = lax.all_gather(video, 'tensor', axis=1, tiled=True)  22.7 us
    dot_general x18, matrix products, absorb(): jnp.einsum('hqk,khd->qhd', weights.astype(jnp.bfloat16), values_split, pr...  18.4 us
    reduce_sum x18, other arithmetic, absorb(): totals = totals * rescale + jnp.sum(weights, axis=-1)  17.8 us
    dot_general x18, matrix products, absorb(): jnp.einsum('qhd,khd->hqk', queries, keys_split, preferred_element_type=jn...  14.6 us
  transfers between devices with their start and end apart: 4, of which 4 were waited for; matrix products, arithmetic and copies ran while one was open for 6% of the time, Pallas kernels for 0%

commit v1 on v0

v1 whole, which is shorter than its diff:
```python
import math

import jax
import jax.numpy as jnp
import numpy as np
from jax import lax
from jax.experimental import pallas as pl
from jax.experimental.pallas import tpu as pltpu
from jax.sharding import PartitionSpec as P

D = 3072
HEAD_DIM = 128
LOCAL_HEADS = 3
ROWS = 272
WIDTH = LOCAL_HEADS * HEAD_DIM
FEAT = 768
TEXT = 256
EPSILON = 1e-06
EXP_FACTOR = math.log2(math.e) / math.sqrt(HEAD_DIM)

FRESH = TEXT
OTHERS = TEXT + ROWS
AT = {1: OTHERS, 7: OTHERS + ROWS, 2: OTHERS + 2 * ROWS, 6: OTHERS + 3 * ROWS,
      3: OTHERS + 4 * ROWS, 5: OTHERS + 5 * ROWS, 4: OTHERS + 6 * ROWS}
EARLY = OTHERS + 4 * ROWS
OWN_STALE = OTHERS + 7 * ROWS
KEYS = OTHERS + 8 * ROWS

HALVES = ((0, 144), (144, 128))

R_SIB, R_PART, R_FWD, R_KV, R_Q, R_WO, R_RS, R_ATT = 0, 2, 4, 6, 22, 31, 35, 51
N_RECV = 54
N_SEND = 64
N_LOCAL = 16


def pair_rates():
    pairs = HEAD_DIM // 2
    frame = HEAD_DIM // 16
    high = (pairs - frame) // 2
    wide = pairs - frame - high
    rates = np.concatenate(
        [256.0 ** (-np.arange(n, dtype=np.float64) / n) for n in (frame, high, wide)]
    )
    return np.repeat(rates, 2).astype(np.float32)[None, :]


def kernel(
    video, pos, count, shift, scale, gate, wq, wk, wv, wout, q_gain, k_gain, sk, sv, tk, tv, rates,
    mixed, fk, fv,
    vb, nb, wqb, wkb, wvb, kb, vvb, qb, cosb, sinb, ob, st, so, ss, ro, rs, wob, atb,
    ssem, rsem, lsem,
):
    f32 = jnp.float32
    p = lax.axis_index("patch")
    t = lax.axis_index("tensor")
    x = p // 16
    z = (p // 2) % 8
    yh = p % 2
    yl = t // 2
    c = t % 2
    turn = 2 * yl
    u = (x - turn + 7) % 4
    ring_place = u * (1 - yh) + (7 - u) * yh

    def along_z(step):
        return x * 16 + ((z + step + 8) % 8) * 2 + yh

    def around(step):
        place = (ring_place + step + 8) % 8
        nyh = place // 4
        nu = place * (1 - nyh) + (7 - place) * nyh
        nx = (turn + 1 + nu) % 4
        return nx * 16 + z * 2 + nyh

    z_next, z_prev, w_next, w_prev = along_z(1), along_z(-1), around(1), around(-1)
    kv_next = (c * z_next + (1 - c) * w_next, t)
    kv_prev = (c * z_prev + (1 - c) * w_prev, t)
    q_next = (c * w_next + (1 - c) * z_next, t)
    q_prev = (c * w_prev + (1 - c) * z_prev, t)
    t_sib = yl * 2 + 1 - c
    t_part = (1 - yl) * 2 + c
    t_far0 = (1 - yl) * 2
    t_far1 = (1 - yl) * 2 + 1
    p_flip = p + 1 - 2 * yh
    sibling = (p, t_sib)
    partner = (p, t_part)
    t_cross = (1 - yl) * 2 + 1 - c

    local = []

    def fetch(src, dst):
        copy = pltpu.make_async_copy(src, dst, lsem.at[len(local)])
        copy.start()
        local.append(copy)
        return copy

    own_video = fetch(video, vb.at[t])
    own_copies = [
        fetch(sk, kb.at[pl.ds(OWN_STALE, ROWS)]),
        fetch(sv, vvb.at[pl.ds(OWN_STALE, ROWS)]),
        fetch(tk, kb.at[pl.ds(0, TEXT)]),
        fetch(tv, vvb.at[pl.ds(0, TEXT)]),
    ]
    got_wq = fetch(wq, wqb)
    got_wk = fetch(wk, wkb)
    got_wv = fetch(wv, wvb)
    got_wo = fetch(wout.at[:, pl.ds(pl.multiple_of(t * FEAT, FEAT), FEAT)], wob.at[t])

    barrier = pltpu.get_barrier_semaphore()
    greeted = (
        sibling, (p, t_far0), (p, t_far1), (p_flip, t_far0), (p_flip, t_far1),
        kv_next, kv_prev, q_next, q_prev,
    )
    for device in greeted:
        pl.semaphore_signal(barrier, inc=1, device_id=device, device_id_type=pl.DeviceIdType.MESH)
    pl.semaphore_wait(barrier, len(greeted))

    sent = []

    def send(src, dst, recv, device):
        index = len(sent)

        def make():
            return pltpu.make_async_remote_copy(
                src_ref=src() if callable(src) else src, dst_ref=dst() if callable(dst) else dst,
                send_sem=ssem.at[index], recv_sem=rsem.at[recv],
                device_id=device, device_id_type=pl.DeviceIdType.MESH,
            )

        sent.append(make)
        make().start()

    def arrived(dst, recv):
        pltpu.make_async_copy(dst, dst, rsem.at[recv]).wait()

    for half, (r0, n) in enumerate(HALVES):
        send(video.at[pl.ds(r0, n)], vb.at[t, pl.ds(r0, n)], R_PART + half, partner)
    for half, (r0, n) in enumerate(HALVES):
        send(video.at[pl.ds(r0, n)], vb.at[t, pl.ds(r0, n)], R_SIB + half, sibling)

    def kv_slot(buffer, d):
        return buffer.at[pl.ds(AT[d], ROWS)]

    send(sk, kv_slot(kb, 7), R_KV + 14, kv_next)
    send(sk, kv_slot(kb, 1), R_KV + 2, kv_prev)
    send(sv, kv_slot(vvb, 7), R_KV + 15, kv_next)
    send(sv, kv_slot(vvb, 1), R_KV + 3, kv_prev)

    def kv_pass(came, going, target, buffer, which):
        arrived(kv_slot(buffer, came), R_KV + 2 * came + which)
        if going is not None:
            send(kv_slot(buffer, came), kv_slot(buffer, going), R_KV + 2 * going + which, target)

    row_id = lax.broadcasted_iota(jnp.int32, (ROWS, ROWS), 0)
    col_id = lax.broadcasted_iota(jnp.int32, (ROWS, ROWS), 1)
    place = jnp.sum(jnp.where(row_id == col_id, pos[...].astype(f32), 0.0), axis=1, keepdims=True)
    frame = jnp.floor((place + 0.5) * (1.0 / 3600.0))
    within = place - 3600.0 * frame
    high = jnp.floor((within + 0.5) * (1.0 / 80.0))
    across = within - 80.0 * high
    lane = lax.broadcasted_iota(jnp.int32, (ROWS, HEAD_DIM), 1)
    angle = jnp.where(lane < 16, frame, jnp.where(lane < 72, high, across)) * rates[...]
    even = lane % 2 == 0
    cosb[...] = jnp.cos(angle)
    sine = jnp.sin(angle)
    sinb[...] = jnp.where(even, -sine, sine)

    def normalise(r0, n):
        blocks = [vb[f, r0 : r0 + n, :].astype(f32) for f in range(4)]
        mean = sum(jnp.sum(b, axis=1, keepdims=True) for b in blocks) * (1.0 / D)
        spread = sum(jnp.sum((b - mean) ** 2, axis=1, keepdims=True) for b in blocks) * (1.0 / D)
        rstd = lax.rsqrt(spread + EPSILON)
        for f in range(4):
            cols = slice(f * FEAT, (f + 1) * FEAT)
            nb[r0 : r0 + n, cols] = (
                (blocks[f] - mean) * rstd * (1.0 + scale[:, cols]) + shift[:, cols]
            ).astype(jnp.bfloat16)

    def rows_of(slot, half):
        r0, n = HALVES[half]
        return vb.at[slot, pl.ds(r0, n)]

    own_video.wait()
    for half in range(2):
        arrived(rows_of(t_part, half), R_PART + half)
        send(rows_of(t_part, half), rows_of(t_part, half), R_FWD + half, sibling)
        if half == 0:
            kv_pass(7, 6, kv_next, kb, 0)
            kv_pass(1, 2, kv_prev, kb, 0)
            kv_pass(7, 6, kv_next, vvb, 1)
            kv_pass(1, 2, kv_prev, vvb, 1)
    for half in range(2):
        arrived(rows_of(t_sib, half), R_SIB + half)
        arrived(rows_of(t_cross, half), R_FWD + half)
        normalise(*HALVES[half])

    def project(weight, gain, target):
        flat = jnp.dot(nb[...], weight[...], preferred_element_type=f32)
        for h in range(LOCAL_HEADS):
            hs = slice(h * HEAD_DIM, (h + 1) * HEAD_DIM)
            v = flat[:, hs]
            v = v * lax.rsqrt(jnp.mean(v * v, axis=1, keepdims=True) + EPSILON) * gain[...]
            other = jnp.where(even, pltpu.roll(v, HEAD_DIM - 1, 1), pltpu.roll(v, 1, 1))
            target[:, hs] = (v * cosb[...] + other * sinb[...]).astype(jnp.bfloat16)

    got_wq.wait()
    project(wqb, q_gain, qb.at[0])
    send(qb.at[0], qb.at[7], R_Q + 7, q_next)
    send(qb.at[0], qb.at[1], R_Q + 1, q_prev)

    send(
        wout.at[:, pl.ds(pl.multiple_of(t_sib * FEAT, FEAT), FEAT)], wob.at[t], R_WO + t, sibling
    )
    send(
        wout.at[:, pl.ds(pl.multiple_of(t_far0 * FEAT, FEAT), FEAT)], wob.at[t], R_WO + t, (p, t_far0)
    )
    send(
        wout.at[:, pl.ds(pl.multiple_of(t_far1 * FEAT, FEAT), FEAT)], wob.at[t], R_WO + t,
        (p_flip, t_far1),
    )

    kv_pass(6, 5, kv_next, kb, 0)
    kv_pass(2, 3, kv_prev, kb, 0)
    kv_pass(6, 5, kv_next, vvb, 1)
    kv_pass(2, 3, kv_prev, vvb, 1)

    got_wk.wait()
    project(wkb, k_gain, kb.at[pl.ds(FRESH, ROWS)])
    got_wv.wait()
    vvb[FRESH : FRESH + ROWS, :] = jnp.dot(nb[...], wvb[...], preferred_element_type=f32).astype(
        jnp.bfloat16
    )
    out_k = fetch(kb.at[pl.ds(FRESH, ROWS)], fk)
    out_v = fetch(vvb.at[pl.ds(FRESH, ROWS)], fv)
    for copy in own_copies:
        copy.wait()

    def scores_of(j, h, k0, n):
        hs = slice(h * HEAD_DIM, (h + 1) * HEAD_DIM)
        return lax.dot_general(
            qb[j, :, hs], kb[k0 : k0 + n, hs], (((1,), (1,)), ((), ())), preferred_element_type=f32
        )

    def product(weights, h, k0, n):
        hs = slice(h * HEAD_DIM, (h + 1) * HEAD_DIM)
        return jnp.dot(
            weights.astype(jnp.bfloat16), vvb[k0 : k0 + n, hs], preferred_element_type=f32
        )

    def keep(j, h, top, total, summed):
        ob[j, :, h * HEAD_DIM : (h + 1) * HEAD_DIM] = summed
        st[j, 0:ROWS, h : h + 1] = top
        st[j, 0:ROWS, 3 + h : 4 + h] = total

    text_rows = lax.broadcasted_iota(jnp.int32, (1, EARLY), 1)
    live = (text_rows < count[0]) | (text_rows >= TEXT)
    for h in range(LOCAL_HEADS):
        scores = jnp.where(live, scores_of(0, h, 0, EARLY), -1e30)
        top = jnp.max(scores, axis=1, keepdims=True)
        weights = jnp.exp2((scores - top) * EXP_FACTOR)
        keep(0, h, top, jnp.sum(weights, axis=1, keepdims=True), product(weights, h, 0, EARLY))

    kv_pass(5, 4, kv_next, kb, 0)
    kv_pass(3, 4, kv_prev, vvb, 1)
    kv_pass(5, None, None, vvb, 1)
    kv_pass(3, None, None, kb, 0)

    def q_pass(came, going, target):
        arrived(qb.at[came], R_Q + came)
        if going is not None:
            send(lambda: qb.at[came], lambda: qb.at[going], R_Q + going, target)

    q_pass(7, 6, q_next)
    q_pass(1, 2, q_prev)
    kv_pass(4, None, None, kb, 0)
    kv_pass(4, None, None, vvb, 1)

    def merge(j, slot, r0, n):
        rows = slice(r0, r0 + n)
        stats = jnp.transpose(rs[slot])[rows, :]
        for h in range(LOCAL_HEADS):
            hs = slice(h * HEAD_DIM, (h + 1) * HEAD_DIM)
            top_a, top_b = st[j, rows, h : h + 1], stats[:, h : h + 1]
            total_a, total_b = st[j, rows, 3 + h : 4 + h], stats[:, 3 + h : 4 + h]
            top = jnp.maximum(top_a, top_b)
            part_a = jnp.exp2((top_a - top) * EXP_FACTOR)
            part_b = jnp.exp2((top_b - top) * EXP_FACTOR)
            ob[j, rows, hs] = ob[j, rows, hs] * part_a + ro[slot, rows, hs].astype(f32) * part_b
            st[j, rows, h : h + 1] = top
            st[j, rows, 3 + h : 4 + h] = total_a * part_a + total_b * part_b

    def pack(j):
        so[j] = ob[j].astype(jnp.bfloat16)
        ss[j] = jnp.transpose(st[j])[0:8, :]

    def received(slot, r0=0, n=ROWS):
        arrived(ro.at[slot, pl.ds(r0, n)], R_RS + 2 * slot)
        arrived(rs.at[slot], R_RS + 2 * slot + 1)

    def emit(j, slot, target, r0=0, n=ROWS):
        send(
            lambda: so.at[j, pl.ds(r0, n)], lambda: ro.at[slot, pl.ds(r0, n)], R_RS + 2 * slot,
            target,
        )
        send(lambda: ss.at[j], lambda: rs.at[slot], R_RS + 2 * slot + 1, target)

    st[...] = jnp.where(
        lax.broadcasted_iota(jnp.int32, st.shape, 0) == 0, st[...], jnp.zeros(st.shape, f32)
    )

    def step(i, order):
        j = order % 8

        @pl.when(i == 1)
        def _():
            q_pass(6, 5, q_next)
            q_pass(2, 3, q_prev)

        @pl.when(i == 2)
        def _():
            arrived(qb.at[5], R_Q + 5)
            send(
                lambda: qb.at[5, pl.ds(0, 144)], lambda: qb.at[4, pl.ds(0, 144)], R_Q + 4, q_next
            )
            arrived(qb.at[3], R_Q + 3)
            send(
                lambda: qb.at[3, pl.ds(144, 128)], lambda: qb.at[4, pl.ds(144, 128)], R_Q + 8, q_prev
            )

        @pl.when(i == 3)
        def _():
            arrived(qb.at[4, pl.ds(0, 144)], R_Q + 4)
            arrived(qb.at[4, pl.ds(144, 128)], R_Q + 8)

        for h in range(LOCAL_HEADS):
            scores = scores_of(j, h, OTHERS, 8 * ROWS)
            top = jnp.max(scores, axis=1, keepdims=True)
            weights = jnp.exp2((scores - top) * EXP_FACTOR)
            keep(
                j, h, top, jnp.sum(weights, axis=1, keepdims=True),
                product(weights, h, OTHERS, 8 * ROWS),
            )

        @pl.when(i == 3)
        def _():
            pack(4)
            emit(4, 3, q_next, 0, 144)
            emit(4, 5, q_prev, 144, 128)

        @pl.when(i == 4)
        def _():
            received(3, 0, 144)
            merge(3, 3, 0, 144)
            pack(3)
            emit(3, 2, q_next)
            received(5, 144, 128)
            merge(5, 5, 144, 128)
            pack(5)
            emit(5, 6, q_prev)

        @pl.when(i == 5)
        def _():
            received(2)
            merge(2, 2, 0, ROWS)
            pack(2)
            emit(2, 1, q_next)

        @pl.when(i == 6)
        def _():
            received(6)
            merge(6, 6, 0, ROWS)
            pack(6)
            emit(6, 7, q_prev)
            received(1)
            merge(1, 1, 0, ROWS)
            pack(1)
            emit(1, 0, q_next)

        return order // 8

    lax.fori_loop(0, 7, step, jnp.int32(0o6254371))

    for h in range(LOCAL_HEADS):
        hs = slice(h * HEAD_DIM, (h + 1) * HEAD_DIM)
        n = OWN_STALE - EARLY
        scores = scores_of(0, h, EARLY, n)
        before = st[0, 0:ROWS, h : h + 1]
        top = jnp.maximum(before, jnp.max(scores, axis=1, keepdims=True))
        weights = jnp.exp2((scores - top) * EXP_FACTOR)
        old = jnp.exp2((before - top) * EXP_FACTOR)
        total = st[0, 0:ROWS, 3 + h : 4 + h] * old + jnp.sum(weights, axis=1, keepdims=True)
        keep(0, h, top, total, ob[0, :, hs] * old + product(weights, h, EARLY, n))

    received(7)
    merge(7, 7, 0, ROWS)
    pack(7)
    emit(7, 4, q_prev)
    received(0)
    merge(0, 0, 0, ROWS)
    received(4)
    merge(0, 4, 0, ROWS)

    for h in range(LOCAL_HEADS):
        hs = slice(h * HEAD_DIM, (h + 1) * HEAD_DIM)
        atb[t, :, hs] = (ob[0, :, hs] / st[0, 0:ROWS, 3 + h : 4 + h]).astype(jnp.bfloat16)

    send(atb.at[t], atb.at[t], R_ATT + 1, partner)
    send(atb.at[t], atb.at[t], R_ATT, sibling)
    got_wo.wait()
    for slot in (t_sib, t_far0, t_far1):
        arrived(wob.at[slot], R_WO + slot)

    def term(slot):
        return jnp.dot(atb[slot], wob[slot], preferred_element_type=f32)

    branch = term(t)
    arrived(atb.at[t_sib], R_ATT)
    branch = branch + term(t_sib)
    arrived(atb.at[t_part], R_ATT + 1)
    send(atb.at[t_part], atb.at[t_part], R_ATT + 2, sibling)
    branch = branch + term(t_part)
    arrived(atb.at[t_cross], R_ATT + 2)
    branch = branch + term(t_cross)
    mixed[...] = vb[t].astype(f32) + gate[...] * branch

    out_k.wait()
    out_v.wait()
    for make in sent:
        make().wait_send()


def shards(
    video, positions, text_count, mod_shift, mod_scale, gate, w_query, w_key, w_value, w_out,
    q_gain, k_gain, stale_keys, stale_values, text_keys, text_values,
):
    bf16, f32 = jnp.bfloat16, jnp.float32
    vmem = pl.BlockSpec(memory_space=pltpu.VMEM)
    smem = pl.BlockSpec(memory_space=pltpu.SMEM)
    hbm = pl.BlockSpec(memory_space=pl.ANY)
    return pl.pallas_call(
        kernel,
        out_shape=(
            jax.ShapeDtypeStruct((ROWS, FEAT), f32),
            jax.ShapeDtypeStruct((ROWS, WIDTH), bf16),
            jax.ShapeDtypeStruct((ROWS, WIDTH), bf16),
        ),
        in_specs=[
            hbm, vmem, smem, vmem, vmem, vmem, hbm, hbm, hbm, hbm, vmem, vmem, hbm, hbm, hbm, hbm,
            vmem,
        ],
        out_specs=(vmem, hbm, hbm),
        scratch_shapes=[
            pltpu.VMEM((4, ROWS, FEAT), bf16),
            pltpu.VMEM((ROWS, D), bf16),
            pltpu.VMEM((D, WIDTH), bf16),
            pltpu.VMEM((D, WIDTH), bf16),
            pltpu.VMEM((D, WIDTH), bf16),
            pltpu.VMEM((KEYS, WIDTH), bf16),
            pltpu.VMEM((KEYS, WIDTH), bf16),
            pltpu.VMEM((8, ROWS, WIDTH), bf16),
            pltpu.VMEM((ROWS, HEAD_DIM), f32),
            pltpu.VMEM((ROWS, HEAD_DIM), f32),
            pltpu.VMEM((8, ROWS, WIDTH), f32),
            pltpu.VMEM((8, 384, HEAD_DIM), f32),
            pltpu.VMEM((8, ROWS, WIDTH), bf16),
            pltpu.VMEM((8, 8, 384), f32),
            pltpu.VMEM((8, ROWS, WIDTH), bf16),
            pltpu.VMEM((8, 8, 384), f32),
            pltpu.VMEM((4, WIDTH, FEAT), bf16),
            pltpu.VMEM((4, ROWS, WIDTH), bf16),
            pltpu.SemaphoreType.DMA((N_SEND,)),
            pltpu.SemaphoreType.DMA((N_RECV,)),
            pltpu.SemaphoreType.DMA((N_LOCAL,)),
        ],
        compiler_params=pltpu.CompilerParams(
            collective_id=0, has_side_effects=True, vmem_limit_bytes=60 * 1024 * 1024
        ),
        name="attention_half",
    )(
        video,
        positions.reshape(1, ROWS),
        text_count,
        mod_shift.reshape(1, D),
        mod_scale.reshape(1, D),
        gate.reshape(1, FEAT),
        w_query,
        w_key,
        w_value,
        w_out,
        q_gain.reshape(1, HEAD_DIM),
        k_gain.reshape(1, HEAD_DIM),
        stale_keys,
        stale_values,
        text_keys,
        text_values,
        jnp.asarray(pair_rates()),
    )


def solution(mesh):
    return jax.shard_map(
        shards,
        mesh=mesh,
        in_specs=(
            P("patch", "tensor"),
            P("patch"),
            P(),
            P(),
            P(),
            P("tensor"),
            P(None, "tensor"),
            P(None, "tensor"),
            P(None, "tensor"),
            P("tensor", None),
            P(),
            P(),
            P("patch", "tensor"),
            P("patch", "tensor"),
            P(None, "tensor"),
            P(None, "tensor"),
        ),
        out_specs=(P("patch", "tensor"), P("patch", "tensor"), P("patch", "tensor")),
        check_vma=False,
    )
```

time: 628 us -> 119 us (0.19)
  waiting for transfers between devices: 376 us -> 0 us
  local copies, waits for them, and re-layouts: 143 us -> 7.88 us
  Pallas kernels: 0 us -> 109 us
  matrix products: 45.3 us -> 0 us
  other arithmetic: 43.9 us -> 0 us
  between operations: 14.7 us -> 1.29 us
    all_gather x3 -> x0, waiting for transfers between devices: 350 us -> none  [the longest x1 178 us: shards(): lax.all_gather(stale_values, 'patch', axis=0, tiled=True)]
    dynamic_slice x68 -> x0, local copies, waits for them, and re-layouts: 119 us -> none  [absorb_blocks(): lax.scan(advance, state, (key_blocks, value_blocks, offsets))]
    pallas_call x0 -> x1, Pallas kernels: none -> 109 us  [shards(): pl.pallas_call(kernel, out_shape=(jax.ShapeDtypeStruct((ROWS, FEAT), f32)...]
    dot_general x40 -> x0, matrix products: 45.3 us -> none  [the longest x18 18.4 us: absorb(): jnp.einsum('hqk,khd->qhd', weights.astype(jnp.bfloat16), values_split, pr...]
    reduce_scatter x1 -> x0, waiting for transfers between devices: 23.8 us -> none  [shards(): lax.psum_scatter(partial_terms.astype(jnp.bfloat16), 'tensor', scatter_di...]
    reduce_sum x22 -> x0, other arithmetic: 20.9 us -> none  [the longest x18 17.8 us: absorb(): totals = totals * rescale + jnp.sum(weights, axis=-1)]
    or x17 -> x0, other arithmetic: 11.1 us -> none  [advance(): live = (index_rows < own_start) | (index_rows >= own_start + own_rows)]
    while x120 -> x0, local copies, waits for them, and re-layouts: 8.23 us -> none
  transfers between devices with their start and end apart: 4 -> 0, of which waited for: 4 -> 0; matrix products, arithmetic and copies ran while one was open for 6% -> 0% of each run, Pallas kernels for 0% -> 0%
where the time goes in v1:
time: 119 us
  Pallas kernels  109 us (92%)
  local copies, waits for them, and re-layouts  7.88 us (7%)
  between operations  1.29 us (1%)
    pallas_call x1, Pallas kernels, shards(): pl.pallas_call(kernel, out_shape=(jax.ShapeDtypeStruct((ROWS, FEAT), f32)...  109 us
    unnamed x3, local copies, waits for them, and re-layouts  5.37 us

profile of v1, /device:TPU:3, one launch (start us, length us, event | category | flops | bytes accessed | tf_op | source)
XLA Modules:
  0.0 118.6 jit_solution(3426696001010534811)
XLA Ops:
  1.3 1.2 %reshape.24.pos = s32[1,272]{1,0:T(1,128)} reshape(s32[272]{0:T(512)} %param.18) | data formatting | bytes 2176 | tf_op jit(solution)/shard_map/reshape | solution.py:482
  2.5 1.3 %reshape.27.gate = f32[1,768]{1,0:T(1,128)} reshape(f32[768]{0:T(1024)} %param.22) | data formatting | bytes 6144 | tf_op jit(solution)/shard_map/reshape | solution.py:486
  3.8 109.4 %attention_half.1 = (f32[272,768]{1,0:T(8,128)}, bf16[272,384]{1,0:T(8,128)(2,1)}, bf16[272,384]{1,0:T(8,128)(2,1)}) custom-call(bf16[272,768]{1,0:T(8,128)(2,1)} %video.1, s32[1,272]{1,0:T(1,128)} %reshape.24.pos, s32[1]{0:T(128)S(6)} %copy.23.count, f32[1,3072]{1,0:T(1,128)} %bitcast.4, f32[1,3072]{1,0:T(1,128)} %bitcast.5, f32[1,768]{1,0:T(1,128)} %reshape.27.gate, ...), custom_call_target="tpu_custom_call" | custom-call | tf_op jit(solution)/shard_map/attention_half/pallas_call | solution.py:441
  113.2 2.1 %copy.24 = f32[272,768]{1,0:T(8,128)} copy(f32[272,768]{1,0:T(8,128)} %get-tuple-element.6) | data formatting | bytes 1671168
  115.3 1.6 %copy.25 = bf16[272,384]{1,0:T(8,128)(2,1)} copy(bf16[272,384]{1,0:T(8,128)(2,1)} %get-tuple-element.7) | data formatting | bytes 417792
  117.0 1.6 %copy.26 = bf16[272,384]{1,0:T(8,128)(2,1)} copy(bf16[272,384]{1,0:T(8,128)(2,1)} %get-tuple-element.8) | data formatting | bytes 417792

commit v2 on v1

v2 whole, which is shorter than its diff:
```python
import functools
import math

import jax
import jax.numpy as jnp
import numpy as np
from jax import lax
from jax.experimental import pallas as pl
from jax.experimental.pallas import tpu as pltpu
from jax.sharding import PartitionSpec as P

D = 3072
HEAD_DIM = 128
LOCAL_HEADS = 3
ROWS = 272
WIDTH = LOCAL_HEADS * HEAD_DIM
FEAT = 768
TEXT = 256
EPSILON = 1e-06
EXP_FACTOR = math.log2(math.e) / math.sqrt(HEAD_DIM)

NEAR = TEXT
FRESH = NEAR + 4 * ROWS
FAR = FRESH + ROWS
OWN_STALE = FAR + 3 * ROWS
KEYS = OWN_STALE + ROWS
SPAN = 4 * ROWS

HALVES = ((0, 144), (144, 128))

STEPS = (
    (0, 0), (1, 0), (2, 0), (3, 0), (4, 0), (1, 1), (2, 1), (5, 0),
    (5, 1), (6, 0), (6, 1), (7, 0), (7, 1), (3, 1), (4, 1), (0, 1),
)
Z_STEP = {1: -1, 2: 1, 3: -2, 4: 2, 5: -3, 6: 3, 7: 4}
X_STEP = {1: (-1, 0), 2: (1, 0), 3: (2, 0), 4: (0, 1), 5: (-1, 1), 6: (1, 1), 7: (2, 1)}


def digits(values, base):
    total = 0
    for value in reversed(values):
        total = total * base + value
    return total


def step_codes(first):
    part = STEPS[first : first + 8]
    return (
        digits([slot for slot, _ in part], 8),
        digits([half for _, half in part], 2),
        digits([Z_STEP.get(slot, 0) + 3 for slot, _ in part], 8),
        digits([X_STEP.get(slot, (0, 0))[0] + 1 + 4 * X_STEP.get(slot, (0, 0))[1] for slot, _ in part], 8),
    )


R_SIB, R_PART, R_FWD, R_KV, R_Q, R_WO, R_RS, R_ATT = 0, 2, 4, 6, 22, 30, 34, 50
N_RECV = 53
N_SEND = 64
N_LOCAL = 16


def pair_rates():
    pairs = HEAD_DIM // 2
    frame = HEAD_DIM // 16
    high = (pairs - frame) // 2
    wide = pairs - frame - high
    rates = np.concatenate(
        [256.0 ** (-np.arange(n, dtype=np.float64) / n) for n in (frame, high, wide)]
    )
    return np.repeat(rates, 2).astype(np.float32)[None, :]


def kernel(
    video, pos, count, shift, scale, gate, wq, wk, wv, wout, q_gain, k_gain, sk, sv, tk, tv, rates,
    mixed, fk, fv,
    vb, nb, wqb, wkb, wvb, kb, vvb, qb, posb, cosb, sinb, sb, ob, tops, sums, stp, so, ss, ro, rs, wob, atb,
    ssem, osem, rsem, lsem,
):
    f32 = jnp.float32
    bf16 = jnp.bfloat16
    p = lax.axis_index("patch")
    t = lax.axis_index("tensor")
    x = p // 16
    z = (p // 2) % 8
    yh = p % 2
    yl = t // 2
    c = t % 2

    def along_z(step):
        return x * 16 + ((z + step + 8) % 8) * 2 + yh

    def along_x(step, flip):
        return ((x + step + 4) % 4) * 16 + z * 2 + yh + flip * (1 - 2 * yh)

    on_z = (along_z(1), along_z(-1), along_z(2), along_z(-2))
    on_x = (along_x(1, 0), along_x(-1, 0), along_x(2, 0), along_x(0, 1))
    k1, k2, k3, k4 = ((c * a + (1 - c) * b, t) for a, b in zip(on_z, on_x))
    q1, q2, q3, q4 = ((c * b + (1 - c) * a, t) for a, b in zip(on_z, on_x))
    t_sib = yl * 2 + 1 - c
    t_part = (1 - yl) * 2 + c
    t_cross = (1 - yl) * 2 + 1 - c
    t_far0 = (1 - yl) * 2
    t_far1 = (1 - yl) * 2 + 1
    p_flip = p + 1 - 2 * yh
    sibling = (p, t_sib)
    partner = (p, t_part)

    local = []

    def fetch(src, dst):
        copy = pltpu.make_async_copy(src, dst, lsem.at[len(local)])
        copy.start()
        local.append(copy)
        return copy

    own_video = fetch(video, vb.at[t])
    own_copies = [
        fetch(sk, kb.at[pl.ds(OWN_STALE, ROWS)]),
        fetch(sv, vvb.at[pl.ds(OWN_STALE, ROWS)]),
    ]
    text_copies = [fetch(tk, kb.at[pl.ds(0, TEXT)]), fetch(tv, vvb.at[pl.ds(0, TEXT)])]
    got_wq = fetch(wq, wqb)
    got_wk = fetch(wk, wkb)
    got_wv = fetch(wv, wvb)
    got_wo = fetch(wout.at[:, pl.ds(pl.multiple_of(t * FEAT, FEAT), FEAT)], wob.at[t])

    barrier = pltpu.get_barrier_semaphore()
    greeted = [sibling, (p, t_far0), (p, t_far1), (p_flip, t_far0), (p_flip, t_far1)]
    greeted += [(along_z(step), t) for step in Z_STEP.values()]
    greeted += [(along_x(*step), t) for step in X_STEP.values()]
    for device in greeted:
        pl.semaphore_signal(barrier, inc=1, device_id=device, device_id_type=pl.DeviceIdType.MESH)
    pl.semaphore_wait(barrier, len(greeted))

    sent = []

    def send(src, dst, recv, device):
        index = len(sent)

        def make():
            return pltpu.make_async_remote_copy(
                src_ref=src() if callable(src) else src, dst_ref=dst() if callable(dst) else dst,
                send_sem=ssem.at[index], recv_sem=rsem.at[recv],
                device_id=device, device_id_type=pl.DeviceIdType.MESH,
            )

        sent.append(make)
        make().start()

    def arrived(dst, recv):
        pltpu.make_async_copy(dst, dst, rsem.at[recv]).wait()

    for half, (r0, n) in enumerate(HALVES):
        send(video.at[pl.ds(r0, n)], vb.at[t, pl.ds(r0, n)], R_PART + half, partner)
    for half, (r0, n) in enumerate(HALVES):
        send(video.at[pl.ds(r0, n)], vb.at[t, pl.ds(r0, n)], R_SIB + half, sibling)

    def place_of(slot):
        return NEAR + (slot - 1) * ROWS if slot < 5 else FAR + (slot - 5) * ROWS

    def kv_slot(buffer, slot):
        return buffer.at[pl.ds(place_of(slot), ROWS)]

    def kv_arrived(slot):
        arrived(kv_slot(kb, slot), R_KV + 2 * slot)
        arrived(kv_slot(vvb, slot), R_KV + 2 * slot + 1)

    def kv_send(buffer, which, row, slot, device):
        src = buffer.at[pl.ds(pl.multiple_of(row, 16), ROWS)]
        send(src, kv_slot(buffer, slot), R_KV + 2 * slot + which, device)

    for which, own in enumerate((sk, sv)):
        buffer = (kb, vvb)[which]
        send(own, kv_slot(buffer, 1), R_KV + 2 + which, k1)
        send(own, kv_slot(buffer, 2), R_KV + 4 + which, k2)

    def spread(r, carry):
        posb[pl.ds(r, 1), :] = jnp.full((1, HEAD_DIM), pos[r], jnp.int32)
        return carry

    lax.fori_loop(0, ROWS, spread, 0)
    place = posb[...].astype(f32)
    frame = jnp.floor((place + 0.5) * (1.0 / 3600.0))
    within = place - 3600.0 * frame
    high = jnp.floor((within + 0.5) * (1.0 / 80.0))
    across = within - 80.0 * high
    lane = lax.broadcasted_iota(jnp.int32, (ROWS, HEAD_DIM), 1)
    angle = jnp.where(lane < 16, frame, jnp.where(lane < 72, high, across)) * rates[...]
    even = lane % 2 == 0
    cosb[...] = jnp.cos(angle)
    sine = jnp.sin(angle)
    sinb[...] = jnp.where(even, -sine, sine)
    stp[...] = jnp.zeros(stp.shape, f32)

    def normalise(r0, n):
        blocks = [vb[f, r0 : r0 + n, :].astype(f32) for f in range(4)]
        mean = sum(jnp.sum(b, axis=1, keepdims=True) for b in blocks) * (1.0 / D)
        spread = sum(jnp.sum((b - mean) ** 2, axis=1, keepdims=True) for b in blocks) * (1.0 / D)
        rstd = lax.rsqrt(spread + EPSILON)
        for f in range(4):
            cols = slice(f * FEAT, (f + 1) * FEAT)
            nb[r0 : r0 + n, cols] = (
                (blocks[f] - mean) * rstd * (1.0 + scale[:, cols]) + shift[:, cols]
            ).astype(bf16)

    def rows_of(slot, half):
        r0, n = HALVES[half]
        return vb.at[slot, pl.ds(r0, n)]

    own_video.wait()
    for copy in own_copies:
        copy.wait()
    for half in range(2):
        arrived(rows_of(t_part, half), R_PART + half)
        send(rows_of(t_part, half), rows_of(t_part, half), R_FWD + half, sibling)
        if half == 0:
            kv_arrived(1)
            kv_arrived(2)
            near_a = c * place_of(1) + (1 - c) * OWN_STALE
            near_b = c * place_of(2) + (1 - c) * OWN_STALE
            to_a = (c * k1[0] + (1 - c) * k3[0], t)
            to_b = (c * k2[0] + (1 - c) * k4[0], t)
            for which, buffer in enumerate((kb, vvb)):
                kv_send(buffer, which, near_a, 3, to_a)
                kv_send(buffer, which, near_b, 4, to_b)
    for half in range(2):
        arrived(rows_of(t_sib, half), R_SIB + half)
        arrived(rows_of(t_cross, half), R_FWD + half)
        normalise(*HALVES[half])

    def project(weight, gain, target):
        flat = jnp.dot(nb[...], weight[...], preferred_element_type=f32)
        for h in range(LOCAL_HEADS):
            hs = slice(h * HEAD_DIM, (h + 1) * HEAD_DIM)
            v = flat[:, hs]
            v = v * lax.rsqrt(jnp.mean(v * v, axis=1, keepdims=True) + EPSILON) * gain[...]
            other = jnp.where(even, pltpu.roll(v, HEAD_DIM - 1, 1), pltpu.roll(v, 1, 1))
            target[:, hs] = (v * cosb[...] + other * sinb[...]).astype(bf16)

    got_wq.wait()
    project(wqb, q_gain, qb.at[0])
    for slot, device in ((1, q1), (2, q2), (3, q3), (4, q4)):
        send(qb.at[0], qb.at[slot], R_Q + slot, device)

    kv_arrived(3)
    kv_arrived(4)
    far_a = c * place_of(3) + (1 - c) * place_of(4)
    to_v = (c * k4[0] + (1 - c) * k3[0], t)
    kv_send(kb, 0, far_a, 5, k1)
    kv_send(kb, 0, place_of(4), 6, k2)
    kv_send(vvb, 1, far_a, 5, k1)
    kv_send(vvb, 1, place_of(4), 6, k2)
    kv_send(kb, 0, far_a, 7, k3)
    kv_send(vvb, 1, place_of(4), 7, to_v)

    got_wk.wait()
    project(wkb, k_gain, kb.at[pl.ds(FRESH, ROWS)])
    got_wv.wait()
    vvb[FRESH : FRESH + ROWS, :] = jnp.dot(nb[...], wvb[...], preferred_element_type=f32).astype(bf16)
    out_k = fetch(kb.at[pl.ds(FRESH, ROWS)], fk)
    out_v = fetch(vvb.at[pl.ds(FRESH, ROWS)], fv)
    for copy in text_copies:
        copy.wait()

    def heads(h):
        return slice(h * HEAD_DIM, (h + 1) * HEAD_DIM)

    def tiles(array):
        return [
            array[:, i : min(i + HEAD_DIM, array.shape[1])] for i in range(0, array.shape[1], HEAD_DIM)
        ]

    def join(op, wide, tile):
        n = tile.shape[1]
        if n == HEAD_DIM:
            return op(wide, tile)
        return jnp.concatenate([op(wide[:, :n], tile), wide[:, n:]], axis=1)

    def row_top(scores):
        parts = tiles(scores)
        top = parts[0]
        for part in parts[1:]:
            top = join(jnp.maximum, top, part)
        return jnp.broadcast_to(jnp.max(top, axis=1, keepdims=True), (ROWS, HEAD_DIM))

    def weigh(scores, top, total):
        weights = [
            jnp.exp2((part - top[:, : part.shape[1]]) * EXP_FACTOR) for part in tiles(scores)
        ]
        for part in weights:
            total = join(jnp.add, total, part)
        return jnp.concatenate([part.astype(bf16) for part in weights], axis=1), total

    def scores_of(j, h, k0, n):
        return lax.dot_general(
            qb[j, :, heads(h)], kb[pl.ds(k0, n), heads(h)], (((1,), (1,)), ((), ())),
            preferred_element_type=f32,
        )

    def product(weights, h, k0, n):
        return jnp.dot(weights, vvb[pl.ds(k0, n), heads(h)], preferred_element_type=f32)

    live = lax.broadcasted_iota(jnp.int32, (1, TEXT), 1) < count[0]
    for h in range(LOCAL_HEADS):
        scores = jnp.where(live, scores_of(0, h, 0, TEXT), -1e30)
        top = row_top(scores)
        weights, total = weigh(scores, top, jnp.zeros((ROWS, HEAD_DIM), f32))
        ob[0, :, heads(h)] = product(weights, h, 0, TEXT)
        tops[0, h] = top
        sums[0, h] = total

    def q_arrived(slot):
        arrived(qb.at[slot], R_Q + slot)

    def half_step(j, k0, first):
        def score(h):
            scores = scores_of(j, h, k0, SPAN)
            sb[h % 2] = scores
            return row_top(scores)

        seen = score(0)
        for h in range(LOCAL_HEADS):
            before = jnp.where(first, -1e30, tops[j, h])
            top = jnp.maximum(before, seen)
            old = jnp.exp2((before - top) * EXP_FACTOR)
            if h + 1 < LOCAL_HEADS:
                seen = score(h + 1)
            weights, total = weigh(sb[h % 2], top, jnp.where(first, 0.0, sums[j, h]) * old)
            ob[j, :, heads(h)] = (
                jnp.where(first, 0.0, ob[j, :, heads(h)]) * old + product(weights, h, k0, SPAN)
            )
            tops[j, h] = top
            sums[j, h] = total

    column = lax.broadcasted_iota(jnp.int32, (ROWS, HEAD_DIM), 1)

    def pack(j):
        stats = jnp.zeros((ROWS, HEAD_DIM), f32)
        for h in range(LOCAL_HEADS):
            stats = jnp.where(column == h, tops[j, h], stats)
            stats = jnp.where(column == 3 + h, jnp.sum(sums[j, h], axis=1, keepdims=True), stats)
        stp[0:ROWS, :] = stats
        ss[j] = jnp.transpose(stp[...])[0:8, :]

    def give_back(j, device):
        return [
            pltpu.make_async_remote_copy(
                src_ref=source.at[j], dst_ref=target.at[j], send_sem=osem.at[2 * j + k],
                recv_sem=rsem.at[R_RS + 2 * j + k], device_id=device, device_id_type=pl.DeviceIdType.MESH,
            )
            for k, (source, target) in enumerate(((so, ro), (ss, rs)))
        ]

    far_q = (1 - c) * 3 + c * 4
    wo_recv = R_WO + t

    def step(i, codes):
        slots, parts, z_steps, x_steps, group = codes
        n = group * 8 + i
        j = slots % 8
        part = parts % 2

        for when, slot in ((1, 1), (2, 2), (7, 5), (9, 6), (11, 7)):
            pl.when(n == when)(functools.partial(q_arrived, slot))

        @pl.when(n == 3)
        def _():
            q_arrived(3)
            q_arrived(4)
            send(lambda: qb.at[far_q], lambda: qb.at[5], R_Q + 5, q1)
            send(lambda: qb.at[4], lambda: qb.at[6], R_Q + 6, q2)
            send(lambda: qb.at[far_q], lambda: qb.at[7], R_Q + 7, q3)

        @pl.when(n == 5)
        def _():
            for slot in (5, 6, 7):
                kv_arrived(slot)
            for user, device in ((t_sib, sibling), (t_far0, (p, t_far0)), (t_far1, (p_flip, t_far1))):
                send(
                    lambda user=user: wout.at[:, pl.ds(pl.multiple_of(user * FEAT, FEAT), FEAT)],
                    lambda: wob.at[t], wo_recv, device,
                )

        k0 = NEAR + part * (FAR - NEAR) - (n // 15) * ROWS
        half_step(j, pl.multiple_of(k0, 16), jnp.logical_and(part == 0, n > 0))

        @pl.when(part == 1)
        def _():
            pack(j)

        @pl.when(jnp.logical_and(part == 1, n < 15))
        def _():
            so[j] = ob[j].astype(bf16)
            shift_z = z_steps % 8 - 3
            shift_x = x_steps % 4 - 1
            flip = (x_steps // 4) % 2
            owner = (1 - c) * along_z(shift_z) + c * along_x(shift_x, flip)
            for copy in give_back(j, (owner, t)):
                copy.start()

        return slots // 8, parts // 2, z_steps // 8, x_steps // 8, group

    first_codes, later_codes = step_codes(0), step_codes(8)

    def eight(group, carry):
        codes = tuple(a + group * (b - a) for a, b in zip(first_codes, later_codes))
        lax.fori_loop(0, 8, step, codes + (group,))
        return carry

    lax.fori_loop(0, 2, eight, 0)

    for slot in range(1, 8):
        arrived(ro.at[slot], R_RS + 2 * slot)
        arrived(rs.at[slot], R_RS + 2 * slot + 1)
    stats = [ss[0]] + [rs[slot] for slot in range(1, 8)]
    top = stats[0][0:3]
    for part in stats[1:]:
        top = jnp.maximum(top, part[0:3])
    shares = [jnp.exp2((part[0:3] - top) * EXP_FACTOR) for part in stats]
    total = sum(share * part[3:6] for share, part in zip(shares, stats))
    blank = jnp.zeros((5, 384), f32)
    rows = [jnp.concatenate([share / total, blank], axis=0) for share in shares]
    rows.append(jnp.zeros((64, 384), f32))
    weight = jnp.transpose(jnp.concatenate(rows, axis=0))[0:ROWS]
    for h in range(LOCAL_HEADS):
        summed = ob[0, :, heads(h)] * weight[:, h : h + 1]
        for slot in range(1, 8):
            summed += ro[slot, :, heads(h)].astype(f32) * weight[:, 8 * slot + h : 8 * slot + h + 1]
        atb[t, :, heads(h)] = summed.astype(bf16)

    send(atb.at[t], atb.at[t], R_ATT + 1, partner)
    send(atb.at[t], atb.at[t], R_ATT, sibling)
    got_wo.wait()
    for slot in (t_sib, t_far0, t_far1):
        arrived(wob.at[slot], R_WO + slot)

    def term(slot):
        return jnp.dot(atb[slot], wob[slot], preferred_element_type=f32)

    branch = term(t)
    arrived(atb.at[t_sib], R_ATT)
    branch = branch + term(t_sib)
    arrived(atb.at[t_part], R_ATT + 1)
    send(atb.at[t_part], atb.at[t_part], R_ATT + 2, sibling)
    branch = branch + term(t_part)
    arrived(atb.at[t_cross], R_ATT + 2)
    branch = branch + term(t_cross)
    mixed[...] = vb[t].astype(f32) + gate[...][None, :] * branch

    out_k.wait()
    out_v.wait()
    for make in sent:
        make().wait_send()
    for slot in range(1, 8):
        for copy in give_back(slot, (p, t_sib)):
            copy.wait_send()


def hand_over(*refs):
    sources, targets, held, sems = refs[:3], refs[3:6], refs[6:9], refs[9]
    inward = [pltpu.make_async_copy(a, b, sems.at[i]) for i, (a, b) in enumerate(zip(sources, held))]
    outward = [
        pltpu.make_async_copy(a, b, sems.at[3 + i]) for i, (a, b) in enumerate(zip(held, targets))
    ]
    for copy in inward:
        copy.start()
    for first, second in zip(inward, outward):
        first.wait()
        second.start()
    for copy in outward:
        copy.wait()


def shards(
    video, positions, text_count, mod_shift, mod_scale, gate, w_query, w_key, w_value, w_out,
    q_gain, k_gain, stale_keys, stale_values, text_keys, text_values,
):
    bf16, f32 = jnp.bfloat16, jnp.float32
    vmem = pl.BlockSpec(memory_space=pltpu.VMEM)
    smem = pl.BlockSpec(memory_space=pltpu.SMEM)
    hbm = pl.BlockSpec(memory_space=pl.ANY)
    outs = (
        jax.ShapeDtypeStruct((ROWS, FEAT), f32),
        jax.ShapeDtypeStruct((ROWS, WIDTH), bf16),
        jax.ShapeDtypeStruct((ROWS, WIDTH), bf16),
    )
    made = pl.pallas_call(
        kernel,
        out_shape=outs,
        in_specs=[
            hbm, smem, smem, vmem, vmem, vmem, hbm, hbm, hbm, hbm, vmem, vmem, hbm, hbm, hbm, hbm,
            vmem,
        ],
        out_specs=(vmem, hbm, hbm),
        scratch_shapes=[
            pltpu.VMEM((4, ROWS, FEAT), bf16),
            pltpu.VMEM((ROWS, D), bf16),
            pltpu.VMEM((D, WIDTH), bf16),
            pltpu.VMEM((D, WIDTH), bf16),
            pltpu.VMEM((D, WIDTH), bf16),
            pltpu.VMEM((KEYS, WIDTH), bf16),
            pltpu.VMEM((KEYS, WIDTH), bf16),
            pltpu.VMEM((8, ROWS, WIDTH), bf16),
            pltpu.VMEM((ROWS, HEAD_DIM), jnp.int32),
            pltpu.VMEM((ROWS, HEAD_DIM), f32),
            pltpu.VMEM((ROWS, HEAD_DIM), f32),
            pltpu.VMEM((2, ROWS, SPAN), f32),
            pltpu.VMEM((8, ROWS, WIDTH), f32),
            pltpu.VMEM((8, LOCAL_HEADS, ROWS, HEAD_DIM), f32),
            pltpu.VMEM((8, LOCAL_HEADS, ROWS, HEAD_DIM), f32),
            pltpu.VMEM((384, HEAD_DIM), f32),
            pltpu.VMEM((8, ROWS, WIDTH), bf16),
            pltpu.VMEM((8, 8, 384), f32),
            pltpu.VMEM((8, ROWS, WIDTH), bf16),
            pltpu.VMEM((8, 8, 384), f32),
            pltpu.VMEM((4, WIDTH, FEAT), bf16),
            pltpu.VMEM((4, ROWS, WIDTH), bf16),
            pltpu.SemaphoreType.DMA((N_SEND,)),
            pltpu.SemaphoreType.DMA((16,)),
            pltpu.SemaphoreType.DMA((N_RECV,)),
            pltpu.SemaphoreType.DMA((N_LOCAL,)),
        ],
        compiler_params=pltpu.CompilerParams(
            collective_id=0, has_side_effects=True, vmem_limit_bytes=60 * 1024 * 1024
        ),
        name="attention_half",
    )(
        video,
        positions,
        text_count,
        mod_shift.reshape(1, D),
        mod_scale.reshape(1, D),
        gate,
        w_query,
        w_key,
        w_value,
        w_out,
        q_gain.reshape(1, HEAD_DIM),
        k_gain.reshape(1, HEAD_DIM),
        stale_keys,
        stale_values,
        text_keys,
        text_values,
        jnp.asarray(pair_rates()),
    )
    return pl.pallas_call(
        hand_over,
        out_shape=outs,
        in_specs=[hbm] * 3,
        out_specs=(hbm,) * 3,
        scratch_shapes=[pltpu.VMEM(out.shape, out.dtype) for out in outs]
        + [pltpu.SemaphoreType.DMA((6,))],
        compiler_params=pltpu.CompilerParams(vmem_limit_bytes=60 * 1024 * 1024),
        name="hand_over",
    )(*made)


def solution(mesh):
    return jax.shard_map(
        shards,
        mesh=mesh,
        in_specs=(
            P("patch", "tensor"),
            P("patch"),
            P(),
            P(),
            P(),
            P("tensor"),
            P(None, "tensor"),
            P(None, "tensor"),
            P(None, "tensor"),
            P("tensor", None),
            P(),
            P(),
            P("patch", "tensor"),
            P("patch", "tensor"),
            P(None, "tensor"),
            P(None, "tensor"),
        ),
        out_specs=(P("patch", "tensor"), P("patch", "tensor"), P("patch", "tensor")),
        check_vma=False,
    )
```

time: 119 us -> 89.3 us (0.75)
  Pallas kernels: 109 us -> 86.6 us
  local copies, waits for them, and re-layouts: 7.88 us -> 0 us
    pallas_call x1 -> x2, Pallas kernels: 109 us -> 86.6 us  [the longest x1 84.4 us: shards(): pl.pallas_call(kernel, out_shape=outs, in_specs=[hbm, smem, smem, vmem, v...]
    unnamed x3 -> x0, local copies, waits for them, and re-layouts: 5.37 us -> none
    reshape x2 -> x0, local copies, waits for them, and re-layouts: 2.51 us -> none  [the longest x1 1.27 us: shards(): gate.reshape(1, FEAT)]
where the time goes in v2:
time: 89.3 us; the launch traced here: 87.9 us
  Pallas kernels  86.6 us (97%)
  between operations  1.29 us (1%)
    pallas_call x1, Pallas kernels, shards(): pl.pallas_call(kernel, out_shape=outs, in_specs=[hbm, smem, smem, vmem, v...  84.4 us
    pallas_call x1, Pallas kernels, shards(): pl.pallas_call(hand_over, out_shape=outs, in_specs=[hbm] * 3, out_specs=(...  2.23 us

profile of v2, /device:TPU:3, one launch (start us, length us, event | category | flops | bytes accessed | tf_op | source)
XLA Modules:
  0.0 87.9 jit_solution(12837601353481066046)
XLA Ops:
  1.3 84.4 %attention_half.1 = (f32[272,768]{1,0:T(8,128)}, bf16[272,384]{1,0:T(8,128)(2,1)}, bf16[272,384]{1,0:T(8,128)(2,1)}) custom-call(bf16[272,768]{1,0:T(8,128)(2,1)} %video.1, s32[272]{0:T(512)} %pos.1, s32[1]{0:T(128)S(6)} %copy.20.count, f32[1,3072]{1,0:T(1,128)} %bitcast.4, f32[1,3072]{1,0:T(1,128)} %bitcast.5, f32[768]{0:T(1024)} %gate.1, ...), custom_call_target="tpu_custom_call" | custom-call | tf_op jit(solution)/shard_map/attention_half/pallas_call | solution.py:487
  85.7 2.2 %hand_over.1 = (f32[272,768]{1,0:T(8,128)}, bf16[272,384]{1,0:T(8,128)(2,1)}, bf16[272,384]{1,0:T(8,128)(2,1)}) custom-call(f32[272,768]{1,0:T(8,128)} %get-tuple-element.6.refs_0_, bf16[272,384]{1,0:T(8,128)(2,1)} %get-tuple-element.7.refs_1_, bf16[272,384]{1,0:T(8,128)(2,1)} %get-tuple-element.8.refs_2_), custom_call_target="tpu_custom_call" | custom-call | tf_op jit(solution)/shard_map/hand_over/pallas_call | solution.py:546

commit v3 on v2

--- a/solution.py
+++ b/solution.py
@@ -29,8 +29,8 @@
 HALVES = ((0, 144), (144, 128))
 
 STEPS = (
-    (0, 0), (1, 0), (2, 0), (3, 0), (4, 0), (1, 1), (2, 1), (5, 0),
-    (5, 1), (6, 0), (6, 1), (7, 0), (7, 1), (3, 1), (4, 1), (0, 1),
+    (0, 0), (1, 0), (2, 0), (3, 0), (4, 0), (1, 1), (2, 1), (3, 1),
+    (4, 1), (5, 0), (5, 1), (6, 0), (6, 1), (7, 0), (7, 1), (0, 1),
 )
 Z_STEP = {1: -1, 2: 1, 3: -2, 4: 2, 5: -3, 6: 3, 7: 4}
 X_STEP = {1: (-1, 0), 2: (1, 0), 3: (2, 0), 4: (0, 1), 5: (-1, 1), 6: (1, 1), 7: (2, 1)}
@@ -53,8 +53,8 @@
     )
 
 
-R_SIB, R_PART, R_FWD, R_KV, R_Q, R_WO, R_RS, R_ATT = 0, 2, 4, 6, 22, 30, 34, 50
-N_RECV = 53
+R_SIB, R_PART, R_FWD, R_KV, R_Q, R_WO, R_RS, R_ATT = 0, 2, 4, 6, 22, 31, 35, 51
+N_RECV = 54
 N_SEND = 64
 N_LOCAL = 16
 
@@ -73,7 +73,7 @@
 def kernel(
     video, pos, count, shift, scale, gate, wq, wk, wv, wout, q_gain, k_gain, sk, sv, tk, tv, rates,
     mixed, fk, fv,
-    vb, nb, wqb, wkb, wvb, kb, vvb, qb, posb, cosb, sinb, sb, ob, tops, sums, stp, so, ss, ro, rs, wob, atb,
+    vb, nb, wqb, wkv, kb, vvb, qb, posb, cosb, sinb, sb, ob, tops, sums, stp, so, ss, ro, rs, wob, atb,
     ssem, osem, rsem, lsem,
 ):
     f32 = jnp.float32
@@ -105,6 +105,13 @@
     sibling = (p, t_sib)
     partner = (p, t_part)
 
+    barrier = pltpu.get_barrier_semaphore()
+    greeted = [sibling, (p, t_far0), (p, t_far1), (p_flip, t_far0), (p_flip, t_far1)]
+    greeted += [(along_z(step), t) for step in Z_STEP.values()]
+    greeted += [(along_x(*step), t) for step in X_STEP.values()]
+    for device in greeted:
+        pl.semaphore_signal(barrier, inc=1, device_id=device, device_id_type=pl.DeviceIdType.MESH)
+
     local = []
 
     def fetch(src, dst):
@@ -120,59 +127,9 @@
     ]
     text_copies = [fetch(tk, kb.at[pl.ds(0, TEXT)]), fetch(tv, vvb.at[pl.ds(0, TEXT)])]
     got_wq = fetch(wq, wqb)
-    got_wk = fetch(wk, wkb)
-    got_wv = fetch(wv, wvb)
+    got_wk = fetch(wk, wkv.at[:, pl.ds(0, WIDTH)])
+    got_wv = fetch(wv, wkv.at[:, pl.ds(WIDTH, WIDTH)])
     got_wo = fetch(wout.at[:, pl.ds(pl.multiple_of(t * FEAT, FEAT), FEAT)], wob.at[t])
-
-    barrier = pltpu.get_barrier_semaphore()
-    greeted = [sibling, (p, t_far0), (p, t_far1), (p_flip, t_far0), (p_flip, t_far1)]
-    greeted += [(along_z(step), t) for step in Z_STEP.values()]
-    greeted += [(along_x(*step), t) for step in X_STEP.values()]
-    for device in greeted:
-        pl.semaphore_signal(barrier, inc=1, device_id=device, device_id_type=pl.DeviceIdType.MESH)
-    pl.semaphore_wait(barrier, len(greeted))
-
-    sent = []
-
-    def send(src, dst, recv, device):
-        index = len(sent)
-
-        def make():
-            return pltpu.make_async_remote_copy(
-                src_ref=src() if callable(src) else src, dst_ref=dst() if callable(dst) else dst,
-                send_sem=ssem.at[index], recv_sem=rsem.at[recv],
-                device_id=device, device_id_type=pl.DeviceIdType.MESH,
-            )
-
-        sent.append(make)
-        make().start()
-
-    def arrived(dst, recv):
-        pltpu.make_async_copy(dst, dst, rsem.at[recv]).wait()
-
-    for half, (r0, n) in enumerate(HALVES):
-        send(video.at[pl.ds(r0, n)], vb.at[t, pl.ds(r0, n)], R_PART + half, partner)
-    for half, (r0, n) in enumerate(HALVES):
-        send(video.at[pl.ds(r0, n)], vb.at[t, pl.ds(r0, n)], R_SIB + half, sibling)
-
-    def place_of(slot):
-        return NEAR + (slot - 1) * ROWS if slot < 5 else FAR + (slot - 5) * ROWS
-
-    def kv_slot(buffer, slot):
-        return buffer.at[pl.ds(place_of(slot), ROWS)]
-
-    def kv_arrived(slot):
-        arrived(kv_slot(kb, slot), R_KV + 2 * slot)
-        arrived(kv_slot(vvb, slot), R_KV + 2 * slot + 1)
-
-    def kv_send(buffer, which, row, slot, device):
-        src = buffer.at[pl.ds(pl.multiple_of(row, 16), ROWS)]
-        send(src, kv_slot(buffer, slot), R_KV + 2 * slot + which, device)
-
-    for which, own in enumerate((sk, sv)):
-        buffer = (kb, vvb)[which]
-        send(own, kv_slot(buffer, 1), R_KV + 2 + which, k1)
-        send(own, kv_slot(buffer, 2), R_KV + 4 + which, k2)
 
     def spread(r, carry):
         posb[pl.ds(r, 1), :] = jnp.full((1, HEAD_DIM), pos[r], jnp.int32)
@@ -192,6 +149,50 @@
     sinb[...] = jnp.where(even, -sine, sine)
     stp[...] = jnp.zeros(stp.shape, f32)
 
+    pl.semaphore_wait(barrier, len(greeted))
+
+    sent = []
+
+    def send(src, dst, recv, device):
+        index = len(sent)
+
+        def make():
+            return pltpu.make_async_remote_copy(
+                src_ref=src() if callable(src) else src, dst_ref=dst() if callable(dst) else dst,
+                send_sem=ssem.at[index], recv_sem=rsem.at[recv],
+                device_id=device, device_id_type=pl.DeviceIdType.MESH,
+            )
+
+        sent.append(make)
+        make().start()
+
+    def arrived(dst, recv):
+        pltpu.make_async_copy(dst, dst, rsem.at[recv]).wait()
+
+    for half, (r0, n) in enumerate(HALVES):
+        send(video.at[pl.ds(r0, n)], vb.at[t, pl.ds(r0, n)], R_PART + half, partner)
+    for half, (r0, n) in enumerate(HALVES):
+        send(video.at[pl.ds(r0, n)], vb.at[t, pl.ds(r0, n)], R_SIB + half, sibling)
+
+    def place_of(slot):
+        return NEAR + (slot - 1) * ROWS if slot < 5 else FAR + (slot - 5) * ROWS
+
+    def kv_slot(buffer, slot):
+        return buffer.at[pl.ds(place_of(slot), ROWS)]
+
+    def kv_arrived(slot):
+        arrived(kv_slot(kb, slot), R_KV + 2 * slot)
+        arrived(kv_slot(vvb, slot), R_KV + 2 * slot + 1)
+
+    def kv_send(buffer, which, row, slot, device):
+        src = buffer.at[pl.ds(pl.multiple_of(row, 16), ROWS)]
+        send(src, kv_slot(buffer, slot), R_KV + 2 * slot + which, device)
+
+    for which, own in enumerate((sk, sv)):
+        buffer = (kb, vvb)[which]
+        send(own, kv_slot(buffer, 1), R_KV + 2 + which, k1)
+        send(own, kv_slot(buffer, 2), R_KV + 4 + which, k2)
+
     def normalise(r0, n):
         blocks = [vb[f, r0 : r0 + n, :].astype(f32) for f in range(4)]
         mean = sum(jnp.sum(b, axis=1, keepdims=True) for b in blocks) * (1.0 / D)
@@ -207,29 +208,52 @@
         r0, n = HALVES[half]
         return vb.at[slot, pl.ds(r0, n)]
 
+    far_a = c * place_of(3) + (1 - c) * place_of(4)
+    near_a = c * place_of(1) + (1 - c) * OWN_STALE
+    near_b = c * place_of(2) + (1 - c) * OWN_STALE
+    to_a = (c * k1[0] + (1 - c) * k3[0], t)
+    to_b = (c * k2[0] + (1 - c) * k4[0], t)
+
+    def second_round(which):
+        buffer = (kb, vvb)[which]
+        for slot in (1, 2):
+            arrived(kv_slot(buffer, slot), R_KV + 2 * slot + which)
+        kv_send(buffer, which, near_a, 3, to_a)
+        kv_send(buffer, which, near_b, 4, to_b)
+
+    def third_round(which):
+        buffer = (kb, vvb)[which]
+        for slot in (3, 4):
+            arrived(kv_slot(buffer, slot), R_KV + 2 * slot + which)
+        kv_send(buffer, which, far_a, 5, k1)
+        kv_send(buffer, which, place_of(4), 6, k2)
+        if which == 0:
+            kv_send(buffer, which, far_a, 7, k3)
+        else:
+            kv_send(buffer, which, place_of(4), 7, (c * k4[0] + (1 - c) * k3[0], t))
+
+    def pass_features(half):
+        arrived(rows_of(t_part, half), R_PART + half)
+        send(rows_of(t_part, half), rows_of(t_part, half), R_FWD + half, sibling)
+
+    def normalise_half(half):
+        arrived(rows_of(t_sib, half), R_SIB + half)
+        arrived(rows_of(t_cross, half), R_FWD + half)
+        normalise(*HALVES[half])
+
     own_video.wait()
     for copy in own_copies:
         copy.wait()
-    for half in range(2):
-        arrived(rows_of(t_part, half), R_PART + half)
-        send(rows_of(t_part, half), rows_of(t_part, half), R_FWD + half, sibling)
-        if half == 0:
-            kv_arrived(1)
-            kv_arrived(2)
-            near_a = c * place_of(1) + (1 - c) * OWN_STALE
-            near_b = c * place_of(2) + (1 - c) * OWN_STALE
-            to_a = (c * k1[0] + (1 - c) * k3[0], t)
-            to_b = (c * k2[0] + (1 - c) * k4[0], t)
-            for which, buffer in enumerate((kb, vvb)):
-                kv_send(buffer, which, near_a, 3, to_a)
-                kv_send(buffer, which, near_b, 4, to_b)
-    for half in range(2):
-        arrived(rows_of(t_sib, half), R_SIB + half)
-        arrived(rows_of(t_cross, half), R_FWD + half)
-        normalise(*HALVES[half])
-
-    def project(weight, gain, target):
-        flat = jnp.dot(nb[...], weight[...], preferred_element_type=f32)
+    second_round(0)
+    pass_features(0)
+    second_round(1)
+    third_round(0)
+    pass_features(1)
+    normalise_half(0)
+    third_round(1)
+    normalise_half(1)
+
+    def turned(flat, gain, target):
         for h in range(LOCAL_HEADS):
             hs = slice(h * HEAD_DIM, (h + 1) * HEAD_DIM)
             v = flat[:, hs]
@@ -238,25 +262,15 @@
             target[:, hs] = (v * cosb[...] + other * sinb[...]).astype(bf16)
 
     got_wq.wait()
-    project(wqb, q_gain, qb.at[0])
+    turned(jnp.dot(nb[...], wqb[...], preferred_element_type=f32), q_gain, qb.at[0])
     for slot, device in ((1, q1), (2, q2), (3, q3), (4, q4)):
         send(qb.at[0], qb.at[slot], R_Q + slot, device)
 
-    kv_arrived(3)
-    kv_arrived(4)
-    far_a = c * place_of(3) + (1 - c) * place_of(4)
-    to_v = (c * k4[0] + (1 - c) * k3[0], t)
-    kv_send(kb, 0, far_a, 5, k1)
-    kv_send(kb, 0, place_of(4), 6, k2)
-    kv_send(vvb, 1, far_a, 5, k1)
-    kv_send(vvb, 1, place_of(4), 6, k2)
-    kv_send(kb, 0, far_a, 7, k3)
-    kv_send(vvb, 1, place_of(4), 7, to_v)
-
     got_wk.wait()
-    project(wkb, k_gain, kb.at[pl.ds(FRESH, ROWS)])
     got_wv.wait()
-    vvb[FRESH : FRESH + ROWS, :] = jnp.dot(nb[...], wvb[...], preferred_element_type=f32).astype(bf16)
+    flat = jnp.dot(nb[...], wkv[...], preferred_element_type=f32)
+    turned(flat[:, 0:WIDTH], k_gain, kb.at[pl.ds(FRESH, ROWS)])
+    vvb[FRESH : FRESH + ROWS, :] = flat[:, WIDTH:].astype(bf16)
     out_k = fetch(kb.at[pl.ds(FRESH, ROWS)], fk)
     out_v = fetch(vvb.at[pl.ds(FRESH, ROWS)], fv)
     for copy in text_copies:
@@ -353,6 +367,7 @@
 
     far_q = (1 - c) * 3 + c * 4
     wo_recv = R_WO + t
+    q_last = ((1 - c) * q4[0] + c * q3[0], t)
 
     def step(i, codes):
         slots, parts, z_steps, x_steps, group = codes
@@ -360,7 +375,7 @@
         j = slots % 8
         part = parts % 2
 
-        for when, slot in ((1, 1), (2, 2), (7, 5), (9, 6), (11, 7)):
+        for when, slot in ((1, 1), (2, 2), (9, 5), (11, 6)):
             pl.when(n == when)(functools.partial(q_arrived, slot))
 
         @pl.when(n == 3)
@@ -369,7 +384,17 @@
             q_arrived(4)
             send(lambda: qb.at[far_q], lambda: qb.at[5], R_Q + 5, q1)
             send(lambda: qb.at[4], lambda: qb.at[6], R_Q + 6, q2)
-            send(lambda: qb.at[far_q], lambda: qb.at[7], R_Q + 7, q3)
+            for half, (source, device) in enumerate(((far_q, q3), (4, q_last))):
+                r0, rows = HALVES[half]
+                send(
+                    lambda source=source, r0=r0, rows=rows: qb.at[source, pl.ds(r0, rows)],
+                    lambda r0=r0, rows=rows: qb.at[7, pl.ds(r0, rows)], R_Q + 7 + half, device,
+                )
+
+        @pl.when(n == 13)
+        def _():
+            for half, (r0, rows) in enumerate(HALVES):
+                arrived(qb.at[7, pl.ds(r0, rows)], R_Q + 7 + half)
 
         @pl.when(n == 5)
         def _():
@@ -496,8 +521,7 @@
             pltpu.VMEM((4, ROWS, FEAT), bf16),
             pltpu.VMEM((ROWS, D), bf16),
             pltpu.VMEM((D, WIDTH), bf16),
-            pltpu.VMEM((D, WIDTH), bf16),
-            pltpu.VMEM((D, WIDTH), bf16),
+            pltpu.VMEM((D, 2 * WIDTH), bf16),
             pltpu.VMEM((KEYS, WIDTH), bf16),
             pltpu.VMEM((KEYS, WIDTH), bf16),
             pltpu.VMEM((8, ROWS, WIDTH), bf16),

time: 89.3 us -> 85.7 us (0.960)
  Pallas kernels: 86.6 us -> 83.1 us
    pallas_call x1, Pallas kernels: 84.4 us -> 80.9 us  [shards(): pl.pallas_call(kernel, out_shape=outs, in_specs=[hbm, smem, smem, vmem, v...]
where the time goes in v3:
time: 85.7 us; the launch traced here: 84.4 us
  Pallas kernels  83.1 us (97%)
  between operations  1.29 us (2%)
    pallas_call x1, Pallas kernels, shards(): pl.pallas_call(kernel, out_shape=outs, in_specs=[hbm, smem, smem, vmem, v...  80.9 us
    pallas_call x1, Pallas kernels, shards(): pl.pallas_call(hand_over, out_shape=outs, in_specs=[hbm] * 3, out_specs=(...  2.23 us

profile of v3, /device:TPU:3, one launch (start us, length us, event | category | flops | bytes accessed | tf_op | source)
XLA Modules:
  0.0 84.4 jit_solution(4329590327026240956)
XLA Ops:
  1.3 80.9 %attention_half.1 = (f32[272,768]{1,0:T(8,128)}, bf16[272,384]{1,0:T(8,128)(2,1)}, bf16[272,384]{1,0:T(8,128)(2,1)}) custom-call(bf16[272,768]{1,0:T(8,128)(2,1)} %video.1, s32[272]{0:T(512)} %pos.1, s32[1]{0:T(128)S(6)} %copy.20.count, f32[1,3072]{1,0:T(1,128)} %bitcast.4, f32[1,3072]{1,0:T(1,128)} %bitcast.5, f32[768]{0:T(1024)} %gate.1, ...), custom_call_target="tpu_custom_call" | custom-call | tf_op jit(solution)/shard_map/attention_half/pallas_call | solution.py:512
  82.2 2.2 %hand_over.1 = (f32[272,768]{1,0:T(8,128)}, bf16[272,384]{1,0:T(8,128)(2,1)}, bf16[272,384]{1,0:T(8,128)(2,1)}) custom-call(f32[272,768]{1,0:T(8,128)} %get-tuple-element.6.refs_0_, bf16[272,384]{1,0:T(8,128)(2,1)} %get-tuple-element.7.refs_1_, bf16[272,384]{1,0:T(8,128)(2,1)} %get-tuple-element.8.refs_2_), custom_call_target="tpu_custom_call" | custom-call | tf_op jit(solution)/shard_map/hand_over/pallas_call | solution.py:570

commit v4 on v3

--- a/solution.py
+++ b/solution.py
@@ -19,12 +19,13 @@
 EPSILON = 1e-06
 EXP_FACTOR = math.log2(math.e) / math.sqrt(HEAD_DIM)
 
-NEAR = TEXT
-FRESH = NEAR + 4 * ROWS
-FAR = FRESH + ROWS
-OWN_STALE = FAR + 3 * ROWS
-KEYS = OWN_STALE + ROWS
-SPAN = 4 * ROWS
+FRESH = TEXT
+NEAR = FRESH + ROWS
+OWN_STALE = NEAR + 4 * ROWS
+FAR = OWN_STALE + ROWS
+KEYS = FAR + 3 * ROWS
+FIRST_SPAN = 5 * ROWS
+LATER_SPAN = 3 * ROWS
 
 HALVES = ((0, 144), (144, 128))
 
@@ -326,22 +327,25 @@
     def q_arrived(slot):
         arrived(qb.at[slot], R_Q + slot)
 
-    def half_step(j, k0, first):
+    def half_step(j, k0, span, first):
+        def held(empty, state):
+            return state if first is False else jnp.where(first, empty, state)
+
         def score(h):
-            scores = scores_of(j, h, k0, SPAN)
-            sb[h % 2] = scores
+            scores = scores_of(j, h, k0, span)
+            sb[h % 2, :, 0:span] = scores
             return row_top(scores)
 
         seen = score(0)
         for h in range(LOCAL_HEADS):
-            before = jnp.where(first, -1e30, tops[j, h])
+            before = held(-1e30, tops[j, h])
             top = jnp.maximum(before, seen)
             old = jnp.exp2((before - top) * EXP_FACTOR)
             if h + 1 < LOCAL_HEADS:
                 seen = score(h + 1)
-            weights, total = weigh(sb[h % 2], top, jnp.where(first, 0.0, sums[j, h]) * old)
+            weights, total = weigh(sb[h % 2, :, 0:span], top, held(0.0, sums[j, h]) * old)
             ob[j, :, heads(h)] = (
-                jnp.where(first, 0.0, ob[j, :, heads(h)]) * old + product(weights, h, k0, SPAN)
+                held(0.0, ob[j, :, heads(h)]) * old + product(weights, h, k0, span)
             )
             tops[j, h] = top
             sums[j, h] = total
@@ -406,8 +410,14 @@
                     lambda: wob.at[t], wo_recv, device,
                 )
 
-        k0 = NEAR + part * (FAR - NEAR) - (n // 15) * ROWS
-        half_step(j, pl.multiple_of(k0, 16), jnp.logical_and(part == 0, n > 0))
+        @pl.when(part == 0)
+        def _():
+            k0 = FRESH + ((n + 15) // 16) * ROWS
+            half_step(j, pl.multiple_of(k0, 16), FIRST_SPAN, n > 0)
+
+        @pl.when(part == 1)
+        def _():
+            half_step(j, FAR, LATER_SPAN, False)
 
         @pl.when(part == 1)
         def _():
@@ -528,7 +538,7 @@
             pltpu.VMEM((ROWS, HEAD_DIM), jnp.int32),
             pltpu.VMEM((ROWS, HEAD_DIM), f32),
             pltpu.VMEM((ROWS, HEAD_DIM), f32),
-            pltpu.VMEM((2, ROWS, SPAN), f32),
+            pltpu.VMEM((2, ROWS, FIRST_SPAN), f32),
             pltpu.VMEM((8, ROWS, WIDTH), f32),
             pltpu.VMEM((8, LOCAL_HEADS, ROWS, HEAD_DIM), f32),
             pltpu.VMEM((8, LOCAL_HEADS, ROWS, HEAD_DIM), f32),

time: 85.7 us -> 84.1 us (0.981)
  Pallas kernels: 83.1 us -> 81.6 us
    pallas_call x1, Pallas kernels: 80.9 us -> 79.3 us  [shards(): pl.pallas_call(kernel, out_shape=outs, in_specs=[hbm, smem, smem, vmem, v...]
where the time goes in v4:
time: 84.1 us; the launch traced here: 82.9 us
  Pallas kernels  81.6 us (97%)
  between operations  1.29 us (2%)
    pallas_call x1, Pallas kernels, shards(): pl.pallas_call(kernel, out_shape=outs, in_specs=[hbm, smem, smem, vmem, v...  79.3 us
    pallas_call x1, Pallas kernels, shards(): pl.pallas_call(hand_over, out_shape=outs, in_specs=[hbm] * 3, out_specs=(...  2.23 us

profile of v4, /device:TPU:3, one launch (start us, length us, event | category | flops | bytes accessed | tf_op | source)
XLA Modules:
  0.0 82.9 jit_solution(3009330621140092791)
XLA Ops:
  1.3 79.3 %attention_half.1 = (f32[272,768]{1,0:T(8,128)}, bf16[272,384]{1,0:T(8,128)(2,1)}, bf16[272,384]{1,0:T(8,128)(2,1)}) custom-call(bf16[272,768]{1,0:T(8,128)(2,1)} %video.1, s32[272]{0:T(512)} %pos.1, s32[1]{0:T(128)S(6)} %copy.20.count, f32[1,3072]{1,0:T(1,128)} %bitcast.4, f32[1,3072]{1,0:T(1,128)} %bitcast.5, f32[768]{0:T(1024)} %gate.1, ...), custom_call_target="tpu_custom_call" | custom-call | tf_op jit(solution)/shard_map/attention_half/pallas_call | solution.py:522
  80.6 2.2 %hand_over.1 = (f32[272,768]{1,0:T(8,128)}, bf16[272,384]{1,0:T(8,128)(2,1)}, bf16[272,384]{1,0:T(8,128)(2,1)}) custom-call(f32[272,768]{1,0:T(8,128)} %get-tuple-element.6.refs_0_, bf16[272,384]{1,0:T(8,128)(2,1)} %get-tuple-element.7.refs_1_, bf16[272,384]{1,0:T(8,128)(2,1)} %get-tuple-element.8.refs_2_), custom_call_target="tpu_custom_call" | custom-call | tf_op jit(solution)/shard_map/hand_over/pallas_call | solution.py:580

commit v5 on v4

--- a/solution.py
+++ b/solution.py
@@ -55,7 +55,7 @@
 
 
 R_SIB, R_PART, R_FWD, R_KV, R_Q, R_WO, R_RS, R_ATT = 0, 2, 4, 6, 22, 31, 35, 51
-N_RECV = 54
+N_RECV = 57
 N_SEND = 64
 N_LOCAL = 16
 
@@ -457,14 +457,18 @@
     rows = [jnp.concatenate([share / total, blank], axis=0) for share in shares]
     rows.append(jnp.zeros((64, 384), f32))
     weight = jnp.transpose(jnp.concatenate(rows, axis=0))[0:ROWS]
-    for h in range(LOCAL_HEADS):
-        summed = ob[0, :, heads(h)] * weight[:, h : h + 1]
-        for slot in range(1, 8):
-            summed += ro[slot, :, heads(h)].astype(f32) * weight[:, 8 * slot + h : 8 * slot + h + 1]
-        atb[t, :, heads(h)] = summed.astype(bf16)
-
-    send(atb.at[t], atb.at[t], R_ATT + 1, partner)
-    send(atb.at[t], atb.at[t], R_ATT, sibling)
+    for half, (r0, n) in enumerate(HALVES):
+        rows_here = slice(r0, r0 + n)
+        for h in range(LOCAL_HEADS):
+            summed = ob[0, rows_here, heads(h)] * weight[rows_here, h : h + 1]
+            for slot in range(1, 8):
+                factor = weight[rows_here, 8 * slot + h : 8 * slot + h + 1]
+                summed += ro[slot, rows_here, heads(h)].astype(f32) * factor
+            atb[t, rows_here, heads(h)] = summed.astype(bf16)
+        mine = atb.at[t, pl.ds(r0, n)]
+        send(mine, mine, R_ATT + 2 + half, partner)
+        send(mine, mine, R_ATT + half, sibling)
+
     got_wo.wait()
     for slot in (t_sib, t_far0, t_far1):
         arrived(wob.at[slot], R_WO + slot)
@@ -473,12 +477,16 @@
         return jnp.dot(atb[slot], wob[slot], preferred_element_type=f32)
 
     branch = term(t)
-    arrived(atb.at[t_sib], R_ATT)
+    for half, (r0, n) in enumerate(HALVES):
+        arrived(atb.at[t_sib, pl.ds(r0, n)], R_ATT + half)
     branch = branch + term(t_sib)
-    arrived(atb.at[t_part], R_ATT + 1)
-    send(atb.at[t_part], atb.at[t_part], R_ATT + 2, sibling)
+    for half, (r0, n) in enumerate(HALVES):
+        theirs = atb.at[t_part, pl.ds(r0, n)]
+        arrived(theirs, R_ATT + 2 + half)
+        send(theirs, theirs, R_ATT + 4 + half, sibling)
     branch = branch + term(t_part)
-    arrived(atb.at[t_cross], R_ATT + 2)
+    for half, (r0, n) in enumerate(HALVES):
+        arrived(atb.at[t_cross, pl.ds(r0, n)], R_ATT + 4 + half)
     branch = branch + term(t_cross)
     mixed[...] = vb[t].astype(f32) + gate[...][None, :] * branch
 

time: 84.1 us -> 83.8 us (level)
  no operation moved by 1% of the time
where the time goes in v5:
time: 83.8 us; the launch traced here: 82.6 us
  Pallas kernels  81.3 us (97%)
  between operations  1.29 us (2%)
    pallas_call x1, Pallas kernels, shards(): pl.pallas_call(kernel, out_shape=outs, in_specs=[hbm, smem, smem, vmem, v...  79 us
    pallas_call x1, Pallas kernels, shards(): pl.pallas_call(hand_over, out_shape=outs, in_specs=[hbm] * 3, out_specs=(...  2.23 us

profile of v5, /device:TPU:3, one launch (start us, length us, event | category | flops | bytes accessed | tf_op | source)
XLA Modules:
  0.0 82.6 jit_solution(8145785801627714163)
XLA Ops:
  1.3 79.0 %attention_half.1 = (f32[272,768]{1,0:T(8,128)}, bf16[272,384]{1,0:T(8,128)(2,1)}, bf16[272,384]{1,0:T(8,128)(2,1)}) custom-call(bf16[272,768]{1,0:T(8,128)(2,1)} %video.1, s32[272]{0:T(512)} %pos.1, s32[1]{0:T(128)S(6)} %copy.20.count, f32[1,3072]{1,0:T(1,128)} %bitcast.4, f32[1,3072]{1,0:T(1,128)} %bitcast.5, f32[768]{0:T(1024)} %gate.1, ...), custom_call_target="tpu_custom_call" | custom-call | tf_op jit(solution)/shard_map/attention_half/pallas_call | solution.py:530
  80.3 2.2 %hand_over.1 = (f32[272,768]{1,0:T(8,128)}, bf16[272,384]{1,0:T(8,128)(2,1)}, bf16[272,384]{1,0:T(8,128)(2,1)}) custom-call(f32[272,768]{1,0:T(8,128)} %get-tuple-element.6.refs_0_, bf16[272,384]{1,0:T(8,128)(2,1)} %get-tuple-element.7.refs_1_, bf16[272,384]{1,0:T(8,128)(2,1)} %get-tuple-element.8.refs_2_), custom_call_target="tpu_custom_call" | custom-call | tf_op jit(solution)/shard_map/hand_over/pallas_call | solution.py:588
